TPU v7x, 128 devices: a whole 4x4x4 slice. The times are simulated.
128 devices in a mesh: expert: 32 (over y, x, z_lo), tensor: 4 (over z_hi, core).
Axes of the slice: x: 4, y: 4, z: 4 (z_hi: 2, z_lo: 2; z = z_hi * 2 + z_lo), core: 2. Of those that a mesh axis runs over, the one named last changes fastest.
Arguments:
- master: float32 [224, 128, 2048], P('expert', None, 'tensor'), may hold values from -0.0625 to 0.0625
- grad: bfloat16 [224, 128, 2048], P('expert', None, 'tensor'), may hold values from -6 to 6
- moment_one: float32 [224, 128, 2048], P('expert', None, 'tensor'), may hold values from -4 to 4
- moment_two: float32 [224, 128, 2048], P('expert', None, 'tensor'), may hold values from 0.05 to 4
- context: bfloat16 [512, 4096], P('expert', 'tensor'), may hold values from -6 to 6
- out_weight: bfloat16 [4096, 7168], P('tensor', 'expert'), may hold values from -0.09375 to 0.09375
- hidden: bfloat16 [512, 7168], P('expert'), may hold values from -6 to 6
- norm_gain: float32 [7168], replicated, may hold values from 0.25 to 1.75
- route: int32 [512], replicated, may hold values from 0 to 3
- plan: int32 [1024], replicated, may hold values from 0 to 223, as said below
Outputs:
- new_master: float32 [224, 128, 2048], P('expert', None, 'tensor')
- new_first: float32 [224, 128, 2048], P('expert', None, 'tensor')
- new_second: float32 [224, 128, 2048], P('expert', None, 'tensor')
- rollout: bfloat16 [1024, 128, 2048], P('expert', None, 'tensor')
- activation: bfloat16 [512, 2048], P('expert', 'tensor')
Inputs may be any that keep to these rules, and one draw needn't show every extreme that they name: `plan`: entry o * 32 + j names the block in slot j of rollout owner o; block b lies on index b // 7 of expert in training; an owner takes at most 2 of its blocks from one training index.
All inputs are finite; a program needn't handle non-finite values.
Results may differ from a plain program's by a relative error of at most 0.0058.
Values may be sent and summed in bfloat16 or wider, within the bound.
A program may use at most 128 MiB of HBM per device.

v0:
```python
import jax
import jax.numpy as jnp
from jax import lax
from jax.sharding import PartitionSpec as P

CAP = 2


beta_one = 0.9
beta_two = 0.95
bias_one = 1.0 - 0.9**50
bias_two = 1.0 - 0.95**50
learn_rate = 0.0003
decay_rate = 0.1
adam_eps = 1e-08


def shards(
    master, grad, moment_one, moment_two, context, out_weight, hidden, norm_gain, route, plan
):
    gradient = grad.astype(jnp.float32)
    new_first = beta_one * moment_one + (1.0 - beta_one) * gradient
    new_second = beta_two * moment_two + (1.0 - beta_two) * gradient * gradient
    update = (
        new_first / bias_one / (jnp.sqrt(new_second / bias_two) + adam_eps) + decay_rate * master
    )
    new_master = master - learn_rate * update
    cast = new_master.astype(jnp.bfloat16)
    owners = lax.axis_size("expert")
    owner_index = lax.axis_index("expert")
    blk_dev = cast.shape[0]
    block_rows = cast.shape[1]
    columns = cast.shape[2]
    slot_count = plan.shape[0] // owners
    table = plan.reshape(owners, slot_count)
    source = table // blk_dev
    local = table % blk_dev
    positions = jnp.arange(slot_count, dtype=jnp.int32)
    same_source = source[:, :, None] == source[:, None, :]
    before = positions[:, None] > positions[None, :]
    rank = jnp.sum((same_source & before[None, :, :]).astype(jnp.int32), axis=2)
    mine = source == owner_index
    hit = mine[:, :, None] & (rank[:, :, None] == jnp.arange(CAP, dtype=jnp.int32)[None, None, :])
    send_index = jnp.sum(hit.astype(jnp.int32) * local[:, :, None], axis=1)
    send_valid = jnp.any(hit, axis=1).astype(jnp.bfloat16)
    outgoing = jnp.take(cast, send_index.reshape(owners * CAP), axis=0).reshape(
        owners, CAP, block_rows, columns
    )
    outgoing = outgoing * send_valid[:, :, None, None]
    incoming = lax.all_to_all(outgoing, "expert", split_axis=0, concat_axis=0, tiled=True)
    flat_blocks = incoming.reshape(owners * CAP, block_rows, columns)
    wanted = source[owner_index] * CAP + rank[owner_index]
    rollout = jnp.take(flat_blocks, wanted, axis=0)
    projected = jnp.dot(
        lax.all_gather(context, "expert", axis=0, tiled=True),
        out_weight,
        preferred_element_type=jnp.float32,
    )
    partial_attn = lax.all_to_all(projected, "expert", split_axis=0, concat_axis=1, tiled=True)
    attn = lax.psum(partial_attn, "tensor")
    resid = hidden.astype(jnp.float32) + attn
    scale = lax.rsqrt(jnp.mean(resid * resid, axis=1, keepdims=True) + 1e-06)
    normed = (resid * scale * norm_gain[None, :]).astype(jnp.bfloat16)
    gathered = lax.all_gather(normed, "expert", axis=0, tiled=True)
    width = hidden.shape[1]
    blk_e = width // block_rows
    block_ids = owner_index * blk_dev + jnp.arange(blk_dev, dtype=jnp.int32)
    expert_of = block_ids // blk_e
    row_of = block_ids % blk_e
    rows = gathered.reshape(hidden.shape[0] * lax.axis_size("expert"), blk_e, block_rows)
    picked = jnp.take(rows, row_of, axis=1)
    weight = (route[:, None] == expert_of[None, :]).astype(jnp.bfloat16)
    pre = lax.psum_scatter(
        jnp.einsum(
            "tlk,lkf->tf", picked * weight[:, :, None], cast, preferred_element_type=jnp.float32
        ),
        "expert",
        scatter_dimension=0,
        tiled=True,
    )
    activation = jax.nn.silu(pre).astype(jnp.bfloat16)
    return (new_master, new_first, new_second, rollout, activation)


def solution(mesh):
    return jax.shard_map(
        shards,
        mesh=mesh,
        in_specs=(
            P("expert", None, "tensor"),
            P("expert", None, "tensor"),
            P("expert", None, "tensor"),
            P("expert", None, "tensor"),
            P("expert", "tensor"),
            P("tensor", "expert"),
            P("expert", None),
            P(),
            P(),
            P(),
        ),
        out_specs=(
            P("expert", None, "tensor"),
            P("expert", None, "tensor"),
            P("expert", None, "tensor"),
            P("expert", None, "tensor"),
            P("expert", "tensor"),
        ),
        check_vma=False,
    )
```

profile of v0, /device:TPU:0, one launch (start us, length us, event | category | flops | bytes accessed | tf_op | source)
XLA Modules:
  0.0 709.5 jit_solution(10705053660816981654)
XLA Ops:
  7.2 0.7 all-gather.3.cloned.1.call-update
  8.0 155.1 %all-gather.3.cloned.1.call-done = bf16[512,1024]{1,0:T(8,128)(2,1)} async-done(((bf16[16,1024]{1,0:T(8,128)(2,1)}), bf16[512,1024]{1,0:T(8,128)(2,1)}) %all-gather.3.cloned.1.call-update) | async-done | bytes 1048592 | tf_op jit(solution)/shard_map/all_gather | solution.py:55
  163.0 1.7 fusion.16
  164.7 18.2 %all_to_all.24 = f32[32,16,224]{2,1,0:T(8,128)S(1)} all-to-all(f32[32,16,224]{2,1,0:T(8,128)S(1)} %bitcast.26), channel_id=1, replica_groups=mesh['expert'=32,'tensor'=4] {'expert'}, dimensions={0} | all-to-all | bytes 917504 | tf_op jit(solution)/shard_map/all_to_all | solution.py:59
  183.0 0.3 copy.25
  183.3 1.1 all_to_all.21
  184.5 39.3 %all-reduce.2.cloned.1.call-done = f32[16,7168]{1,0:T(8,128)} async-done(((f32[16,7168]{1,0:T(8,128)}), f32[16,7168]{1,0:T(8,128)}) %all-reduce.2.cloned.1.call-update) | async-done | bytes 458768 | tf_op jit(solution)/shard_map/psum | solution.py:60
  223.8 1.2 multiply_reduce_fusion
  225.0 1.8 multiply_convert_fusion
  227.1 0.8 convert_reduce_fusion
  228.1 0.1 select_reduce_fusion
  228.6 5.8 fusion.13
  234.5 5.4 gather_fusion
  239.8 7.5 %select_multiply_fusion = bf16[32,2,128,512]{3,2,1,0:T(8,128)(2,1)} fusion(bf16[32,2,128,512]{3,2,1,0:T(8,128)(2,1)} %bitcast.23, pred[32,2]{1,0:T(8,128)(4,1)S(1)} %copy.21, bf16[32,2]{1,0:T(8,128)(2,1)S(1)} %copy.23), kind=kLoop, calls=%fused_computation.3 | loop fusion | flops 8388608 | bytes 16777408 | tf_op jit(solution)/shard_map/mul | solution.py:49
  247.3 7.5 %all-to-all-start = ((bf16[32,2,128,512]{3,2,1,0:T(8,128)(2,1)}), bf16[32,2,128,512]{3,2,1,0:T(8,128)(2,1)}, u32[]{:S(2)}, u32[]{:S(2)}) async-start(bf16[32,2,128,512]{3,2,1,0:T(8,128)(2,1)} %select_multiply_fusion), calls=%async_computation | async-start | bytes 16777216 | tf_op jit(solution)/shard_map/all_to_all | solution.py:50
  255.1 259.9 %all-gather.5.cloned.1.call-done = bf16[512,7168]{1,0:T(8,128)(2,1)} async-done(((bf16[16,7168]{1,0:T(8,128)(2,1)}), bf16[512,7168]{1,0:T(8,128)(2,1)}) %all-gather.5.cloned.1.call-update) | async-done | bytes 7340048 | tf_op jit(solution)/shard_map/all_gather | solution.py:64
  515.0 10.4 %copy.26 = bf16[512,7168]{0,1:T(8,128)(2,1)} copy(bf16[512,7168]{1,0:T(8,128)(2,1)} %all-gather.5.cloned.1.call-done) | data formatting | bytes 14680064 | tf_op jit(solution)/shard_map/all_gather | solution.py:64
  525.4 10.4 %copy.27 = bf16[512,56,128]{2,0,1:T(8,128)(2,1)} copy(bf16[512,56,128]{0,2,1:T(8,128)(2,1)} %bitcast.24) | data formatting | bytes 14680064 | tf_op jit(solution)/shard_map/reshape | solution.py:70
  535.8 3.8 gather_fusion.2
  539.6 1.7 convolution_bitcast_fusion
  541.4 6.2 gather_fusion.1
  547.6 4.7 broadcast_select_fusion
  552.4 149.2 %reduce-scatter.2.cloned.1.call-done = f32[16,512]{1,0:T(8,128)} async-done(((f32[512,512]{1,0:T(8,128)}), f32[16,512]{1,0:T(8,128)}) %reduce-scatter.2.cloned.1.call-update) | async-done | bytes 32784 | tf_op jit(solution)/shard_map/reduce_scatter | solution.py:73
  701.6 1.4 multiply_convert_fusion.1
  (47 shorter events, 1.2 us)
Async XLA Ops:
  7.2 155.9 %copy-start = (bf16[1024,224]{0,1:T(8,128)(2,1)S(1)}, bf16[1024,224]{0,1:T(8,128)(2,1)}, u32[]{:S(2)}) copy-start(bf16[1024,224]{0,1:T(8,128)(2,1)} %param.15) | copy-start | bytes 1376260
  7.2 155.8 %all-gather.3.cloned.1.call-start = ((), (), s32[]{:S(2)}) async-start(), calls=%async_computation.3 | async-start | bytes 1081344 | tf_op jit(solution)/shard_map/all_gather | solution.py:55
  7.9 215.9 %all-reduce.2.cloned.1.call-start = ((), (), s32[]{:S(2)}) async-start(), calls=%async_computation.4 | async-start | bytes 917504 | tf_op jit(solution)/shard_map/psum | solution.py:60
  164.7 59.1 %copy-start.3 = (bf16[16,7168]{1,0:T(8,128)(2,1)S(1)}, bf16[16,7168]{1,0:T(8,128)(2,1)}, u32[]{:S(2)}) copy-start(bf16[16,7168]{1,0:T(8,128)(2,1)} %param.16) | copy-start | bytes 688132
  183.0 42.0 %copy-start.4 = (f32[7168]{0:T(1024)S(1)}, f32[7168]{0:T(1024)}, u32[]{:S(2)}) copy-start(f32[7168]{0:T(1024)} %param.17) | copy-start | bytes 86020
  183.3 43.6 %copy-start.5 = (s32[1024]{0:T(1024)S(1)}, s32[1024]{0:T(1024)}, u32[]{:S(2)}) copy-start(s32[1024]{0:T(1024)} %param.19) | copy-start | bytes 12292
  183.3 45.3 %copy-start.2 = (f32[7,128,512]{2,1,0:T(8,128)S(1)}, f32[7,128,512]{2,1,0:T(8,128)}, u32[]{:S(2)}) copy-start(f32[7,128,512]{2,1,0:T(8,128)} %param.10) | copy-start | bytes 5505028
  184.4 330.6 %all-gather.5.cloned.1.call-start = ((), (), s32[]{:S(2)}) async-start(), calls=%async_computation.5 | async-start | bytes 7569408 | tf_op jit(solution)/shard_map/all_gather | solution.py:64
  247.3 7.7 %copy-start.6 = (s32[512]{0:T(512)S(1)}, s32[512]{0:T(512)}, u32[]{:S(2)}) copy-start(s32[512]{0:T(512)} %param.18) | copy-start | bytes 6148
  247.3 294.1 %all-to-all-start = ((bf16[32,2,128,512]{3,2,1,0:T(8,128)(2,1)}), bf16[32,2,128,512]{3,2,1,0:T(8,128)(2,1)}, u32[]{:S(2)}, u32[]{:S(2)}) async-start(bf16[32,2,128,512]{3,2,1,0:T(8,128)(2,1)} %select_multiply_fusion), calls=%async_computation | async-start | bytes 16777216 | tf_op jit(solution)/shard_map/all_to_all | solution.py:50
  254.9 446.7 %reduce-scatter.2.cloned.1.call-start = ((), (), s32[]{:S(2)}) async-start(), calls=%async_computation.6 | async-start | bytes 1081344 | tf_op jit(solution)/shard_map/reduce_scatter | solution.py:73
  547.6 155.4 %copy-start.1 = (bf16[1024,224]{0,1:T(8,128)(2,1)S(1)}, bf16[1024,224]{0,1:T(8,128)(2,1)}, u32[]{:S(2)}) copy-start(bf16[1024,224]{0,1:T(8,128)(2,1)} %param.15) | copy-start | bytes 1376260
Sparse Core Ops, SparseCore 0:
  9.7 153.3 all-gather.2
  184.5 39.2 all-reduce.1
  227.0 287.9 all-gather.4
  541.5 160.0 reduce-scatter.1
where the time goes:
time: 711 us; the launch traced here: 710 us
  waiting for transfers between devices  604 us (85%)
  local copies, waits for them, and re-layouts  38.2 us (5%)
  other arithmetic  23.7 us (3%)
  blocking collectives  18.2 us (3%)
  between operations  14 us (2%)
  starting transfers between devices  7.67 us (1%)
    all_gather x1, waiting for transfers between devices, shards(): gathered = lax.all_gather(normed, 'expert', axis=0, tiled=True)  260 us
    all_gather x1, waiting for transfers between devices, shards(): lax.all_gather(context, 'expert', axis=0, tiled=True)  155 us
    reduce_scatter x1, waiting for transfers between devices, shards(): lax.psum_scatter(jnp.einsum('tlk,lkf->tf', picked * weight[:, :, None], c...  149 us
    psum x1, waiting for transfers between devices, shards(): attn = lax.psum(partial_attn, 'tensor')  39.3 us
    all_to_all x1, blocking collectives, shards(): lax.all_to_all(projected, 'expert', split_axis=0, concat_axis=1, tiled=True)  18.2 us
  transfers between devices with their start and end apart: 5, of which 4 were waited for; matrix products, arithmetic and copies ran while one was open for 8% of the time, Pallas kernels for 0%

commit v1 on v0

--- a/solution.py
+++ b/solution.py
@@ -1,10 +1,22 @@
+import functools
+
 import jax
 import jax.numpy as jnp
 from jax import lax
+from jax.experimental import pallas as pl
+from jax.experimental.pallas import tpu as pltpu
 from jax.sharding import PartitionSpec as P
 
+MESH = pl.DeviceIdType.MESH
 CAP = 2
-
+N_E = 32
+N_T = 4
+TOK_DEV = 16
+COLS = 224
+WIDE = 256
+GROUP = 128
+FCOL = 512
+MSG = 640
 
 beta_one = 0.9
 beta_two = 0.95
@@ -13,6 +25,258 @@
 learn_rate = 0.0003
 decay_rate = 0.1
 adam_eps = 1e-08
+
+
+def split_sum(total):
+    high = total.astype(jnp.bfloat16)
+    low = (total - high.astype(jnp.float32)).astype(jnp.bfloat16)
+    return high.astype(jnp.float32), low.astype(jnp.float32)
+
+
+def decode_kernel(
+    ctx, ow, hid, gain, cast, pre_out,
+    ctx_all, ow_wide, hid_send, hid_recv, gain_all, part_send, part_recv, part_own, msg, held, pre_send,
+    s_ctx, r_ctx, s_hid, r_hid, s_part, r_part, s_msg, r_msg, s_held, r_held, s_pre, r_pre, local_sem,
+):
+    e = lax.axis_index("expert")
+    t = lax.axis_index("tensor")
+    y, x, z = e // 8, (e // 2) % 4, e % 2
+
+    barrier = pltpu.get_barrier_semaphore()
+
+    @pl.loop(1, N_E)
+    def _(i):
+        pl.semaphore_signal(barrier, 1, device_id=((e + i) % N_E, t), device_id_type=MESH)
+
+    for j in range(1, N_T):
+        pl.semaphore_signal(barrier, 1, device_id=(e, (t + j) % N_T), device_id_type=MESH)
+    pl.semaphore_wait(barrier, N_E - 1 + N_T - 1)
+
+    def ctx_copy(i):
+        return pltpu.make_async_remote_copy(
+            ctx, ctx_all.at[e], s_ctx.at[i], r_ctx.at[i], device_id=((e + i) % N_E, t), device_id_type=MESH
+        )
+
+    @pl.loop(1, N_E)
+    def _(i):
+        ctx_copy(i).start()
+
+    ctx_all[e] = ctx[...]
+
+    spot = x * 2 + z
+    sends_hidden = y == t
+
+    def hid_copy(i):
+        return pltpu.make_async_remote_copy(
+            hid_send.at[(e + i) % N_E], hid_recv.at[spot], s_hid.at[i], r_hid.at[spot],
+            device_id=((e + i) % N_E, t), device_id_type=MESH,
+        )
+
+    @pl.when(sends_hidden)
+    def _():
+        hid_send[...] = jnp.zeros_like(hid_send)
+        for g in range(N_E):
+            hid_send[g, :, :COLS] = hid[:, g * COLS : (g + 1) * COLS]
+
+        @pl.loop(1, N_E)
+        def _(i):
+            hid_copy(i).start()
+
+        hid_recv[spot] = hid_send[e]
+
+    gain_all[...] = jnp.zeros_like(gain_all)
+    for g in range(N_E):
+        gain_all[g, :, :COLS] = gain[:, g * COLS : (g + 1) * COLS]
+    ow_wide[...] = jnp.zeros_like(ow_wide)
+    ow_wide[:, :COLS] = ow[...]
+
+    @pl.loop(1, N_E)
+    def _(i):
+        ctx_copy(i).wait_recv()
+
+    def projected(group):
+        values = ctx_all[pl.ds(group * 8, 8)].reshape(GROUP, ctx.shape[1])
+        return jnp.dot(values, ow_wide[...], preferred_element_type=jnp.float32)
+
+    def part_copy(j):
+        return pltpu.make_async_remote_copy(
+            part_send.at[j], part_recv.at[j], s_part.at[j], r_part.at[j],
+            device_id=(e, (t + j) % N_T), device_id_type=MESH,
+        )
+
+    for j in (2, 3, 1):
+        part_send[j] = projected((t + j) % N_T).astype(jnp.bfloat16)
+        part_copy(j).start()
+    part_own[...] = projected(t)
+
+    for q in range(8):
+        @pl.when(t * 8 + q != e)
+        def _(q=q):
+            pltpu.make_async_copy(hid_recv.at[q], hid_recv.at[q], r_hid.at[q]).wait()
+
+    resid = part_own[...] + hid_recv[...].reshape(GROUP, WIDE).astype(jnp.float32)
+    for j in (1, 2, 3):
+        part_copy(j).wait_recv()
+        resid = resid + part_recv[j].astype(jnp.float32)
+    high, low = split_sum(jnp.sum(resid * resid, axis=1, keepdims=True))
+    lane = lax.broadcasted_iota(jnp.int32, (GROUP, WIDE), 1)
+    scaled = resid * gain_all[e]
+    scaled = jnp.where(lane == COLS, high, jnp.where(lane == COLS + 1, low, scaled))
+    msg[...] = scaled.astype(jnp.bfloat16)
+
+    spot_in = (x % 2) * 2 + z
+    my_slice = 2 * x + z
+
+    def msg_copy(k):
+        target = k * 8 + 2 * y + x // 2
+        return target, pltpu.make_async_remote_copy(
+            msg, held.at[t, spot_in], s_msg.at[k], r_msg.at[spot_in], device_id=(target, t), device_id_type=MESH
+        )
+
+    for k in range(4):
+        target, copy = msg_copy(k)
+
+        @pl.when(target != e)
+        def _(copy=copy):
+            copy.start()
+
+        @pl.when(target == e)
+        def _():
+            held[t, spot_in] = msg[...]
+
+    for j in range(4):
+        @pl.when(my_slice * 4 + j != e)
+        def _(j=j):
+            pltpu.make_async_copy(held.at[t, j], held.at[t, j], r_msg.at[j]).wait()
+
+    def held_copy(j):
+        return pltpu.make_async_remote_copy(
+            held.at[t], held.at[t], s_held.at[j], r_held.at[j], device_id=(e, (t + j) % N_T), device_id_type=MESH
+        )
+
+    for j in (2, 3, 1):
+        held_copy(j).start()
+
+    def pre_copy(o):
+        return pltpu.make_async_remote_copy(
+            pre_send.at[o], pre_out.at[e], s_pre.at[o], r_pre.at[e], device_id=(o, t), device_id_type=MESH
+        )
+
+    own_copy = pltpu.make_async_copy(pre_send.at[e], pre_out.at[e], local_sem)
+
+    tail_lane = lax.broadcasted_iota(jnp.int32, (GROUP, MSG - FCOL), 1)
+    for j in (0, 1, 2, 3):
+        if j:
+            group = (t + N_T - j) % N_T
+            pltpu.make_async_copy(held.at[group], held.at[group], r_held.at[j]).wait()
+        else:
+            group = t
+        weight = cast[...].reshape(896, FCOL)
+        total = jnp.zeros((GROUP, FCOL), jnp.float32)
+        squares = jnp.zeros((GROUP, 1), jnp.float32)
+        for i in range(4):
+            block = held[group, i]
+            total = total + jnp.dot(
+                block[:, :COLS], weight[i * COLS : (i + 1) * COLS], preferred_element_type=jnp.float32
+            )
+            tail = block[:, GROUP:].astype(jnp.float32)
+            squares = squares + jnp.sum(
+                jnp.where(tail_lane >= COLS - GROUP, tail, 0.0), axis=1, keepdims=True
+            )
+        high, low = split_sum(squares)
+        extra = jnp.where(tail_lane == 0, high, jnp.where(tail_lane == 1, low, 0.0))
+        pre_send[pl.ds(group * 8, 8), :, :FCOL] = total.astype(jnp.bfloat16).reshape(8, TOK_DEV, FCOL)
+        pre_send[pl.ds(group * 8, 8), :, FCOL:] = extra.astype(jnp.bfloat16).reshape(8, TOK_DEV, MSG - FCOL)
+
+        @pl.loop(0, 8)
+        def _(q, group=group):
+            o = group * 8 + q
+
+            @pl.when(o != e)
+            def _():
+                pre_copy(o).start()
+
+            @pl.when(o == e)
+            def _():
+                own_copy.start()
+
+    own_copy.wait()
+
+    @pl.loop(1, N_E)
+    def _(i):
+        source = (e + i) % N_E
+        pltpu.make_async_copy(pre_send.at[source], pre_out.at[source], r_pre.at[source]).wait()
+        pre_copy(source).wait_send()
+        ctx_copy(i).wait_send()
+
+    @pl.when(sends_hidden)
+    def _():
+        @pl.loop(1, N_E)
+        def _(i):
+            hid_copy(i).wait_send()
+
+    for j in (1, 2, 3):
+        part_copy(j).wait_send()
+        held_copy(j).wait_send()
+    for k in range(4):
+        target, copy = msg_copy(k)
+
+        @pl.when(target != e)
+        def _(copy=copy):
+            copy.wait_send()
+
+
+def decode(context, out_weight, hidden, norm_gain, cast):
+    vmem = pl.BlockSpec(memory_space=pltpu.VMEM)
+    dma = pltpu.SemaphoreType.DMA
+    bf16 = jnp.bfloat16
+    return pl.pallas_call(
+        decode_kernel,
+        out_shape=jax.ShapeDtypeStruct((N_E, TOK_DEV, MSG), bf16),
+        in_specs=[vmem] * 5,
+        out_specs=pl.BlockSpec(memory_space=pl.ANY),
+        scratch_shapes=[
+            pltpu.VMEM((N_E, TOK_DEV, context.shape[1]), bf16),
+            pltpu.VMEM((out_weight.shape[0], WIDE), bf16),
+            pltpu.VMEM((N_E, TOK_DEV, WIDE), bf16),
+            pltpu.VMEM((8, TOK_DEV, WIDE), bf16),
+            pltpu.VMEM((N_E, 1, WIDE), jnp.float32),
+            pltpu.VMEM((N_T, GROUP, WIDE), bf16),
+            pltpu.VMEM((N_T, GROUP, WIDE), bf16),
+            pltpu.VMEM((GROUP, WIDE), jnp.float32),
+            pltpu.VMEM((GROUP, WIDE), bf16),
+            pltpu.VMEM((N_T, 4, GROUP, WIDE), bf16),
+            pltpu.VMEM((N_E, TOK_DEV, MSG), bf16),
+            dma((N_E,)), dma((N_E,)), dma((N_E,)), dma((8,)), dma((N_T,)), dma((N_T,)), dma((4,)), dma((4,)),
+            dma((N_T,)), dma((N_T,)), dma((N_E,)), dma((N_E,)), dma,
+        ],
+        compiler_params=pltpu.CompilerParams(
+            collective_id=0, has_side_effects=True, vmem_limit_bytes=40 * 2**20
+        ),
+        cost_estimate=pl.CostEstimate(flops=10**9, bytes_accessed=10**8, transcendentals=0),
+        name="decode",
+    )(context, out_weight, hidden, norm_gain.reshape(1, -1), cast)
+
+
+def finish_kernel(partial, route, out):
+    expert = route[...]
+    pre = jnp.zeros((TOK_DEV, FCOL), jnp.float32)
+    squares = jnp.zeros((TOK_DEV, 1), jnp.float32)
+    for k in range(4):
+        total = jnp.zeros((TOK_DEV, FCOL), jnp.float32)
+        for h in range(8):
+            total = total + partial[k * 8 + h, :, :FCOL].astype(jnp.float32)
+        pre = pre + jnp.where(expert == k, total, 0.0)
+    for h in range(8):
+        squares = squares + jnp.sum(partial[h, :, FCOL:].astype(jnp.float32), axis=1, keepdims=True)
+    pre = pre * lax.rsqrt(squares / (N_E * COLS) + 1e-06)
+    out[...] = (pre / (1.0 + jnp.exp(-pre))).astype(jnp.bfloat16)
+
+
+def finish(partial, route_own):
+    return pl.pallas_call(
+        finish_kernel, out_shape=jax.ShapeDtypeStruct((TOK_DEV, FCOL), jnp.bfloat16), name="finish"
+    )(partial, route_own)
 
 
 def shards(
@@ -42,43 +306,16 @@
     mine = source == owner_index
     hit = mine[:, :, None] & (rank[:, :, None] == jnp.arange(CAP, dtype=jnp.int32)[None, None, :])
     send_index = jnp.sum(hit.astype(jnp.int32) * local[:, :, None], axis=1)
-    send_valid = jnp.any(hit, axis=1).astype(jnp.bfloat16)
     outgoing = jnp.take(cast, send_index.reshape(owners * CAP), axis=0).reshape(
         owners, CAP, block_rows, columns
     )
-    outgoing = outgoing * send_valid[:, :, None, None]
     incoming = lax.all_to_all(outgoing, "expert", split_axis=0, concat_axis=0, tiled=True)
     flat_blocks = incoming.reshape(owners * CAP, block_rows, columns)
     wanted = source[owner_index] * CAP + rank[owner_index]
     rollout = jnp.take(flat_blocks, wanted, axis=0)
-    projected = jnp.dot(
-        lax.all_gather(context, "expert", axis=0, tiled=True),
-        out_weight,
-        preferred_element_type=jnp.float32,
-    )
-    partial_attn = lax.all_to_all(projected, "expert", split_axis=0, concat_axis=1, tiled=True)
-    attn = lax.psum(partial_attn, "tensor")
-    resid = hidden.astype(jnp.float32) + attn
-    scale = lax.rsqrt(jnp.mean(resid * resid, axis=1, keepdims=True) + 1e-06)
-    normed = (resid * scale * norm_gain[None, :]).astype(jnp.bfloat16)
-    gathered = lax.all_gather(normed, "expert", axis=0, tiled=True)
-    width = hidden.shape[1]
-    blk_e = width // block_rows
-    block_ids = owner_index * blk_dev + jnp.arange(blk_dev, dtype=jnp.int32)
-    expert_of = block_ids // blk_e
-    row_of = block_ids % blk_e
-    rows = gathered.reshape(hidden.shape[0] * lax.axis_size("expert"), blk_e, block_rows)
-    picked = jnp.take(rows, row_of, axis=1)
-    weight = (route[:, None] == expert_of[None, :]).astype(jnp.bfloat16)
-    pre = lax.psum_scatter(
-        jnp.einsum(
-            "tlk,lkf->tf", picked * weight[:, :, None], cast, preferred_element_type=jnp.float32
-        ),
-        "expert",
-        scatter_dimension=0,
-        tiled=True,
-    )
-    activation = jax.nn.silu(pre).astype(jnp.bfloat16)
+    partial = decode(context, out_weight, hidden, norm_gain, cast)
+    route_own = lax.dynamic_slice(route, (owner_index * TOK_DEV,), (TOK_DEV,)).reshape(TOK_DEV, 1)
+    activation = finish(partial, route_own)
     return (new_master, new_first, new_second, rollout, activation)
 
 

time: 711 us -> 238 us (0.33)
  the two profiles are of different devices: /device:TPU:0 before, /device:TPU:70 now
where the time goes in v1:
time: 238 us; the launch traced here: 237 us
  Pallas kernels  193 us (81%)
  other arithmetic  20.9 us (9%)
  local copies, waits for them, and re-layouts  13.9 us (6%)
  starting transfers between devices  8.94 us (4%)
    pallas_call x1, Pallas kernels, decode(): pl.pallas_call(decode_kernel, out_shape=jax.ShapeDtypeStruct((N_E, TOK_DE...  191 us
    all_to_all x1, starting transfers between devices, shards(): lax.all_to_all(outgoing, 'expert', split_axis=0, concat_axis=0, tiled=True)  8.94 us
    select_n x2, other arithmetic, shards(): jnp.take(cast, send_index.reshape(owners * CAP), axis=0)  7.48 us
    convert_element_type x1, other arithmetic, shards(): cast = new_master.astype(jnp.bfloat16)  6.42 us
    gather x1, local copies, waits for them, and re-layouts, shards(): rollout = jnp.take(flat_blocks, wanted, axis=0)  6.21 us
    gather x1, local copies, waits for them, and re-layouts, shards(): jnp.take(cast, send_index.reshape(owners * CAP), axis=0)  5.37 us
  transfers between devices with their start and end apart: 1, of which 0 were waited for; matrix products, arithmetic and copies ran while one was open for 0% of the time, Pallas kernels for 81%

profile of v1, /device:TPU:70, one launch (start us, length us, event | category | flops | bytes accessed | tf_op | source)
XLA Modules:
  0.0 237.4 jit_solution(10799631314673089505)
XLA Ops:
  0.6 0.0 copy-start
  0.6 0.7 sign_compare_fusion
  1.3 0.7 broadcast_divide_fusion
  2.0 0.1 ne.56
  2.1 0.1 div.41
  2.2 0.1 rem.33
  2.3 0.8 convert_reduce_fusion
  3.1 0.1 select_reduce_fusion
  3.2 0.1 copy.20
  3.3 0.1 copy.19
  3.4 0.1 reshape.174
  3.5 6.4 %fusion.5 = (bf16[7,128,512]{2,1,0:T(8,128)(2,1)S(1)}, f32[7,128,512]{2,1,0:T(8,128)}, f32[7,128,512]{2,1,0:T(8,128)}, f32[7,128,512]{2,1,0:T(8,128)}) fusion(f32[7,128,512]{2,1,0:T(8,128)} %param.10, bf16[7,128,512]{2,1,0:T(8,128)(2,1)} %param.11, f32[7,128,512]{2,1,0:T(8,128)} %param.12, f32[7,128,512]{2,1,0:T(8,128)} %param.13), kind=kLoop, calls=%fused_computation.33 | loop fusion | flops 7798784 | bytes 12845056 | tf_op jit(solution)/shard_map/convert_element_type | solution.py:292
  10.0 5.4 %gather_fusion = bf16[64,128,512]{2,1,0:T(8,128)(2,1)} fusion(bf16[7,128,512]{2,1,0:T(8,128)(2,1)S(1)} %get-tuple-element.9.cast, s32[1024]{0:T(1024)S(1)} %pad_clamp_fusion.1), kind=kCustom, calls=%fused_computation | custom fusion | bytes 16777472 | tf_op jit(solution)/shard_map/jit(_take)/gather | solution.py:309
  15.3 7.5 %broadcast_select_fusion = bf16[32,2,128,512]{3,2,1,0:T(8,128)(2,1)} fusion(bf16[32,2,128,512]{3,2,1,0:T(8,128)(2,1)} %bitcast.14, pred[32,2]{1,0:T(8,128)(4,1)S(1)} %copy.19), kind=kLoop, calls=%fused_computation.2 | loop fusion | flops 4194304 | bytes 16777280 | tf_op jit(solution)/shard_map/jit(_take)/select_n | solution.py:309
  22.8 8.9 %all-to-all-start = ((bf16[32,2,128,512]{3,2,1,0:T(8,128)(2,1)}), bf16[32,2,128,512]{3,2,1,0:T(8,128)(2,1)}, u32[]{:S(2)}, u32[]{:S(2)}) async-start(bf16[32,2,128,512]{3,2,1,0:T(8,128)(2,1)} %broadcast_select_fusion), calls=%async_computation | async-start | bytes 16777216 | tf_op jit(solution)/shard_map/all_to_all | solution.py:312
  31.8 0.1 dynamic-slice_bitcast_fusion
  31.8 0.7 copy.22.route
  32.5 0.2 copy.21.ow
  32.8 191.1 %decode.1.partial = bf16[32,16,640]{2,1,0:T(8,128)(2,1)S(1)} custom-call(bf16[16,1024]{1,0:T(8,128)(2,1)S(1)} %copy-done.3, bf16[1024,224]{1,0:T(8,128)(2,1)S(1)} %copy.21.ow, bf16[16,7168]{1,0:T(8,128)(2,1)S(1)} %copy-done.2, f32[1,7168]{1,0:T(1,128)S(1)} %bitcast.13, bf16[7,128,512]{2,1,0:T(8,128)(2,1)S(1)} %get-tuple-element.9.cast), custom_call_target="tpu_custom_call" | custom-call | flops 1000000000 | bytes 100000000 | tf_op jit(solution)/shard_map/decode/pallas_call | solution.py:233
  223.8 0.0 copy-start.1
  223.8 0.8 copy-done.1
  224.7 1.8 finish.1
  226.6 6.2 %gather_fusion.1 = bf16[32,128,512]{2,1,0:T(8,128)(2,1)} fusion(bf16[64,128,512]{2,1,0:T(8,128)(2,1)} %bitcast.3, s32[1024]{0:T(1024)S(1)} %pad_clamp_fusion), kind=kCustom, calls=%fused_computation.1 | custom fusion | bytes 8388736 | tf_op jit(solution)/shard_map/jit(_take)/gather | solution.py:315
  232.8 4.7 %broadcast_select_fusion.1 = bf16[32,128,512]{2,1,0:T(8,128)(2,1)} fusion(bf16[32,128,512]{2,1,0:T(8,128)(2,1)} %gather_fusion.1, pred[32]{0:T(512)(128)(4,1)S(1)} %get-tuple-element.5), kind=kLoop, calls=%fused_computation.3 | loop fusion | flops 2097152 | bytes 8388640 | tf_op jit(solution)/shard_map/jit(_take)/select_n | solution.py:315
  (18 shorter events, 0.1 us)
Async XLA Ops:
  0.6 31.1 %copy-start = (s32[512]{0:T(512)S(1)}, s32[512]{0:T(512)}, u32[]{:S(2)}) copy-start(s32[512]{0:T(512)} %param.18) | copy-start | bytes 6148
  22.8 9.7 %copy-start.5 = (bf16[1024,224]{0,1:T(8,128)(2,1)S(1)}, bf16[1024,224]{0,1:T(8,128)(2,1)}, u32[]{:S(2)}) copy-start(bf16[1024,224]{0,1:T(8,128)(2,1)} %param.15) | copy-start | bytes 1376260
  22.8 9.9 %copy-start.2 = (bf16[16,7168]{1,0:T(8,128)(2,1)S(1)}, bf16[16,7168]{1,0:T(8,128)(2,1)}, u32[]{:S(2)}) copy-start(bf16[16,7168]{1,0:T(8,128)(2,1)} %hid.1) | copy-start | bytes 688132
  22.8 9.9 %copy-start.3 = (bf16[16,1024]{1,0:T(8,128)(2,1)S(1)}, bf16[16,1024]{1,0:T(8,128)(2,1)}, u32[]{:S(2)}) copy-start(bf16[16,1024]{1,0:T(8,128)(2,1)} %ctx.1) | copy-start | bytes 98308
  22.8 9.9 %copy-start.4 = (f32[7168]{0:T(1024)S(1)}, f32[7168]{0:T(1024)}, u32[]{:S(2)}) copy-start(f32[7168]{0:T(1024)} %param.17) | copy-start | bytes 86020
  22.8 203.8 %all-to-all-start = ((bf16[32,2,128,512]{3,2,1,0:T(8,128)(2,1)}), bf16[32,2,128,512]{3,2,1,0:T(8,128)(2,1)}, u32[]{:S(2)}, u32[]{:S(2)}) async-start(bf16[32,2,128,512]{3,2,1,0:T(8,128)(2,1)} %broadcast_select_fusion), calls=%async_computation | async-start | bytes 16777216 | tf_op jit(solution)/shard_map/all_to_all | solution.py:312
  223.8 0.8 copy-start.1

commit v2 on v1

v2 whole, which is shorter than its diff:
```python
import functools

import jax
import jax.numpy as jnp
from jax import lax
from jax.experimental import pallas as pl
from jax.experimental.pallas import tpu as pltpu
from jax.sharding import PartitionSpec as P

MESH = pl.DeviceIdType.MESH
CAP = 2
N_E = 32
N_T = 4
TOK_DEV = 16
COLS = 224
WIDE = 256
GROUP = 128
FCOL = 512
MSG = 640
HALF = 64

beta_one = 0.9
beta_two = 0.95
bias_one = 1.0 - 0.9**50
bias_two = 1.0 - 0.95**50
learn_rate = 0.0003
decay_rate = 0.1
adam_eps = 1e-08


def split_sum(total):
    high = total.astype(jnp.bfloat16)
    low = (total - high.astype(jnp.float32)).astype(jnp.bfloat16)
    return high.astype(jnp.float32), low.astype(jnp.float32)


def step_kernel(
    ctx, ow, hid, gain, table, cast, pre_out, roll_a, roll_b,
    ctx_all, ow_wide, hid_send, hid_recv, gain_all, part_send, part_recv, part_own, msg, held, pre_send, *rest
):
    near = (rest[0:7], rest[7:14])
    picked = rest[14:16]
    (
        s_ctx, r_ctx, s_hid, r_hid, s_part, r_part, s_msg, r_msg, s_held, r_held, s_pre, r_pre, local_sem,
        s_near, r_near, s_pick, r_pick, l_pick,
    ) = rest[16:]
    roll = (roll_a, roll_b)
    e = lax.axis_index("expert")
    t = lax.axis_index("tensor")
    y, x, z = e // 8, (e // 2) % 4, e % 2

    barrier = pltpu.get_barrier_semaphore()

    @pl.loop(1, N_E)
    def _(i):
        pl.semaphore_signal(barrier, 1, device_id=((e + i) % N_E, t), device_id_type=MESH)

    for j in range(1, N_T):
        pl.semaphore_signal(barrier, 1, device_id=(e, (t + j) % N_T), device_id_type=MESH)
    pl.semaphore_wait(barrier, N_E - 1 + N_T - 1)

    def at(dy, dx, dz):
        return ((y + dy) % 4) * 8 + ((x + dx) % 4) * 2 + (z + dz) % 2

    def gather_to(half, d, dz=0):
        return at(d, 0, dz) if half == 0 else at(0, d, dz)

    def owner_at(half, d):
        return at(0, d, 0) if half == 0 else at(d, 0, 0)

    def own_rows(half):
        return cast.at[:, pl.ds(half * HALF, HALF)]

    def near_copy(half, step):
        source, place, target = {
            "z": (None, 1, gather_to(half, 0, 1)),
            "own+": (None, 6, gather_to(half, 1)),
            "own-": (None, 2, gather_to(half, 3)),
            "z+": (1, 7, gather_to(half, 1)),
            "z-": (1, 3, gather_to(half, 3)),
            "on+": (6, 4, gather_to(half, 1)),
            "on-": (3, 5, gather_to(half, 3)),
        }[step]
        index = half * 8 + place
        return pltpu.make_async_remote_copy(
            own_rows(half) if source is None else near[half][source - 1], near[half][place - 1],
            s_near.at[index], r_near.at[index], device_id=(target, t), device_id_type=MESH,
        )

    def pick_copy(half, g, d):
        index = half * 24 + g * 3 + d - 1
        return pltpu.make_async_remote_copy(
            picked[half].at[g, d], roll[half].at[4 - d, g], s_pick.at[index], r_pick.at[index],
            device_id=(owner_at(half, d), t), device_id_type=MESH,
        )

    def keep_copy(half, g):
        return pltpu.make_async_copy(picked[half].at[g, 0], roll[half].at[0, g], l_pick.at[half * 8 + g])

    def pick(half, g):
        source = gather_to(half, g // 2, g % 2)
        for d in (1, 3, 2, 0):
            owner = owner_at(half, d)
            for r in range(CAP):
                block = table[(source * N_E + owner) * CAP + r]
                if g == 0:
                    picked[half][g, d, r] = cast[block, pl.ds(half * HALF, HALF)]
                else:
                    picked[half][g, d, r] = near[half][g - 1][block]
            if d:
                pick_copy(half, g, d).start()
            else:
                keep_copy(half, g).start()

    STEPS = ("z", "own+", "own-", "z+", "z-", "on+", "on-")

    def ctx_copy(i):
        return pltpu.make_async_remote_copy(
            ctx, ctx_all.at[e], s_ctx.at[i], r_ctx.at[i], device_id=((e + i) % N_E, t), device_id_type=MESH
        )

    def ctx_start():
        @pl.loop(1, N_E)
        def _(i):
            ctx_copy(i).start()

        ctx_all[e] = ctx[...]

    spot = x * 2 + z
    sends_hidden = y == t

    def hid_copy(i):
        return pltpu.make_async_remote_copy(
            hid_send.at[(e + i) % N_E], hid_recv.at[spot], s_hid.at[i], r_hid.at[spot],
            device_id=((e + i) % N_E, t), device_id_type=MESH,
        )

    def hid_start():
        @pl.when(sends_hidden)
        def _():
            hid_send[...] = jnp.zeros_like(hid_send)
            for g in range(N_E):
                hid_send[g, :, :COLS] = hid[:, g * COLS : (g + 1) * COLS]

            @pl.loop(1, N_E)
            def _(i):
                hid_copy(i).start()

            hid_recv[spot] = hid_send[e]

    def prepare():
        gain_all[...] = jnp.zeros_like(gain_all)
        for g in range(N_E):
            gain_all[g, :, :COLS] = gain[:, g * COLS : (g + 1) * COLS]
        ow_wide[...] = jnp.zeros_like(ow_wide)
        ow_wide[:, :COLS] = ow[...]

    def ctx_wait():
        @pl.loop(1, N_E)
        def _(i):
            ctx_copy(i).wait_recv()

    def projected(group):
        values = ctx_all[pl.ds(group * 8, 8)].reshape(GROUP, ctx.shape[1])
        return jnp.dot(values, ow_wide[...], preferred_element_type=jnp.float32)

    def part_copy(j):
        return pltpu.make_async_remote_copy(
            part_send.at[j], part_recv.at[j], s_part.at[j], r_part.at[j],
            device_id=(e, (t + j) % N_T), device_id_type=MESH,
        )

    def project():
        for j in (2, 3, 1):
            part_send[j] = projected((t + j) % N_T).astype(jnp.bfloat16)
            part_copy(j).start()
        part_own[...] = projected(t)

    def residual():
        for q in range(8):
            @pl.when(t * 8 + q != e)
            def _(q=q):
                pltpu.make_async_copy(hid_recv.at[q], hid_recv.at[q], r_hid.at[q]).wait()

        resid = part_own[...] + hid_recv[...].reshape(GROUP, WIDE).astype(jnp.float32)
        for j in (1, 2, 3):
            part_copy(j).wait_recv()
            resid = resid + part_recv[j].astype(jnp.float32)
        high, low = split_sum(jnp.sum(resid * resid, axis=1, keepdims=True))
        lane = lax.broadcasted_iota(jnp.int32, (GROUP, WIDE), 1)
        scaled = resid * gain_all[e]
        scaled = jnp.where(lane == COLS, high, jnp.where(lane == COLS + 1, low, scaled))
        msg[...] = scaled.astype(jnp.bfloat16)

    spot_in = (x % 2) * 2 + z
    my_slice = 2 * x + z

    def msg_copy(k):
        target = k * 8 + 2 * y + x // 2
        return target, pltpu.make_async_remote_copy(
            msg, held.at[t, spot_in], s_msg.at[k], r_msg.at[spot_in], device_id=(target, t), device_id_type=MESH
        )

    def msg_start():
        for k in range(4):
            target, copy = msg_copy(k)

            @pl.when(target != e)
            def _(copy=copy):
                copy.start()

            @pl.when(target == e)
            def _():
                held[t, spot_in] = msg[...]

    def msg_wait():
        for j in range(4):
            @pl.when(my_slice * 4 + j != e)
            def _(j=j):
                pltpu.make_async_copy(held.at[t, j], held.at[t, j], r_msg.at[j]).wait()

    def held_copy(j):
        return pltpu.make_async_remote_copy(
            held.at[t], held.at[t], s_held.at[j], r_held.at[j], device_id=(e, (t + j) % N_T), device_id_type=MESH
        )

    def held_start():
        for j in (2, 3, 1):
            held_copy(j).start()

    def pre_copy(o):
        return pltpu.make_async_remote_copy(
            pre_send.at[o], pre_out.at[e], s_pre.at[o], r_pre.at[e], device_id=(o, t), device_id_type=MESH
        )

    own_copy = pltpu.make_async_copy(pre_send.at[e], pre_out.at[e], local_sem)

    tail_lane = lax.broadcasted_iota(jnp.int32, (GROUP, MSG - FCOL), 1)

    def expert_rows(j):
        if j:
            group = (t + N_T - j) % N_T
            pltpu.make_async_copy(held.at[group], held.at[group], r_held.at[j]).wait()
        else:
            group = t
        weight = cast[...].reshape(896, FCOL)
        total = jnp.zeros((GROUP, FCOL), jnp.float32)
        squares = jnp.zeros((GROUP, 1), jnp.float32)
        for i in range(4):
            block = held[group, i]
            total = total + jnp.dot(
                block[:, :COLS], weight[i * COLS : (i + 1) * COLS], preferred_element_type=jnp.float32
            )
            tail = block[:, GROUP:].astype(jnp.float32)
            squares = squares + jnp.sum(
                jnp.where(tail_lane >= COLS - GROUP, tail, 0.0), axis=1, keepdims=True
            )
        high, low = split_sum(squares)
        extra = jnp.where(tail_lane == 0, high, jnp.where(tail_lane == 1, low, 0.0))
        pre_send[pl.ds(group * 8, 8), :, :FCOL] = total.astype(jnp.bfloat16).reshape(8, TOK_DEV, FCOL)
        pre_send[pl.ds(group * 8, 8), :, FCOL:] = extra.astype(jnp.bfloat16).reshape(8, TOK_DEV, MSG - FCOL)

        @pl.loop(0, 8)
        def _(q, group=group):
            o = group * 8 + q

            @pl.when(o != e)
            def _():
                pre_copy(o).start()

            @pl.when(o == e)
            def _():
                own_copy.start()

    def finish_decode():
        own_copy.wait()

        @pl.loop(1, N_E)
        def _(i):
            source = (e + i) % N_E
            pltpu.make_async_copy(pre_send.at[source], pre_out.at[source], r_pre.at[source]).wait()
            pre_copy(source).wait_send()
            ctx_copy(i).wait_send()

        @pl.when(sends_hidden)
        def _():
            @pl.loop(1, N_E)
            def _(i):
                hid_copy(i).wait_send()

        for j in (1, 2, 3):
            part_copy(j).wait_send()
            held_copy(j).wait_send()
        for k in range(4):
            target, copy = msg_copy(k)

            @pl.when(target != e)
            def _(copy=copy):
                copy.wait_send()

    ctx_start()
    near_copy(0, "z").start()
    for half in (0, 1):
        near_copy(half, "own+").start()
        near_copy(half, "own-").start()
    hid_start()
    prepare()
    pick(0, 0)
    pick(1, 0)
    ctx_wait()
    project()
    near_copy(1, "z").start()
    near_copy(0, "z").wait_recv()
    near_copy(0, "z+").start()
    near_copy(0, "z-").start()
    residual()
    msg_start()
    near_copy(1, "z").wait_recv()
    near_copy(1, "z+").start()
    near_copy(1, "z-").start()
    for half in (0, 1):
        near_copy(half, "own+").wait_recv()
        near_copy(half, "on+").start()
    pick(0, 1)
    pick(1, 1)
    msg_wait()
    held_start()
    for half in (0, 1):
        near_copy(half, "z-").wait_recv()
        near_copy(half, "on-").start()
    for half in (0, 1):
        pick(half, 6)
    for half in (0, 1):
        near_copy(half, "own-").wait_recv()
        pick(half, 2)
    expert_rows(0)
    expert_rows(1)
    expert_rows(2)
    expert_rows(3)
    for half in (0, 1):
        pick(half, 3)
    for half in (0, 1):
        near_copy(half, "z+").wait_recv()
        pick(half, 7)
    for half in (0, 1):
        near_copy(half, "on+").wait_recv()
        pick(half, 4)
    for half in (0, 1):
        near_copy(half, "on-").wait_recv()
        pick(half, 5)

    finish_decode()
    for half in (0, 1):
        for step in STEPS:
            near_copy(half, step).wait_send()
        for g in range(8):
            keep_copy(half, g).wait()
            for d in (1, 2, 3):
                pick_copy(half, g, d).wait()


def step(context, out_weight, hidden, norm_gain, table, cast):
    vmem = pl.BlockSpec(memory_space=pltpu.VMEM)
    anywhere = pl.BlockSpec(memory_space=pl.ANY)
    dma = pltpu.SemaphoreType.DMA
    bf16 = jnp.bfloat16
    columns = cast.shape[2]
    rolled = jax.ShapeDtypeStruct((4, 8, CAP, HALF, columns), bf16)
    return pl.pallas_call(
        step_kernel,
        out_shape=(jax.ShapeDtypeStruct((N_E, TOK_DEV, MSG), bf16), rolled, rolled),
        in_specs=[vmem] * 4 + [pl.BlockSpec(memory_space=pltpu.SMEM), vmem],
        out_specs=(anywhere,) * 3,
        scratch_shapes=[
            pltpu.VMEM((N_E, TOK_DEV, context.shape[1]), bf16),
            pltpu.VMEM((out_weight.shape[0], WIDE), bf16),
            pltpu.VMEM((N_E, TOK_DEV, WIDE), bf16),
            pltpu.VMEM((8, TOK_DEV, WIDE), bf16),
            pltpu.VMEM((N_E, 1, WIDE), jnp.float32),
            pltpu.VMEM((N_T, GROUP, WIDE), bf16),
            pltpu.VMEM((N_T, GROUP, WIDE), bf16),
            pltpu.VMEM((GROUP, WIDE), jnp.float32),
            pltpu.VMEM((GROUP, WIDE), bf16),
            pltpu.VMEM((N_T, 4, GROUP, WIDE), bf16),
            pltpu.VMEM((N_E, TOK_DEV, MSG), bf16),
            *[pltpu.VMEM((cast.shape[0], HALF, columns), bf16)] * 14,
            *[pltpu.VMEM((8, 4, CAP, HALF, columns), bf16)] * 2,
            dma((N_E,)), dma((N_E,)), dma((N_E,)), dma((8,)), dma((N_T,)), dma((N_T,)), dma((4,)), dma((4,)),
            dma((N_T,)), dma((N_T,)), dma((N_E,)), dma((N_E,)), dma,
            dma((16,)), dma((16,)), dma((48,)), dma((48,)), dma((16,)),
        ],
        compiler_params=pltpu.CompilerParams(
            collective_id=0, has_side_effects=True, vmem_limit_bytes=48 * 2**20
        ),
        name="step",
    )(context, out_weight, hidden, norm_gain.reshape(1, -1), table, cast)


def finish_kernel(place_a, place_b, partial, route, roll_a, roll_b, out, rollout, stage, in_sems, out_sems):
    def fetch(j, half):
        rolled, place = ((roll_a, place_a), (roll_b, place_b))[half]
        return pltpu.make_async_copy(
            rolled.at[place[j]], stage.at[j, pl.ds(half * HALF, HALF)], in_sems.at[2 * j + half]
        )

    def store(j):
        return pltpu.make_async_copy(stage.at[j], rollout.at[j], out_sems.at[j])

    slots = rollout.shape[0]

    @pl.loop(0, slots)
    def _(j):
        fetch(j, 0).start()
        fetch(j, 1).start()

    expert = route[...]
    pre = jnp.zeros((TOK_DEV, FCOL), jnp.float32)
    squares = jnp.zeros((TOK_DEV, 1), jnp.float32)
    for k in range(4):
        total = jnp.zeros((TOK_DEV, FCOL), jnp.float32)
        for h in range(8):
            total = total + partial[k * 8 + h, :, :FCOL].astype(jnp.float32)
        pre = pre + jnp.where(expert == k, total, 0.0)
    for h in range(8):
        squares = squares + jnp.sum(partial[h, :, FCOL:].astype(jnp.float32), axis=1, keepdims=True)
    pre = pre * lax.rsqrt(squares / (N_E * COLS) + 1e-06)
    out[...] = (pre / (1.0 + jnp.exp(-pre))).astype(jnp.bfloat16)

    @pl.loop(0, slots)
    def _(j):
        fetch(j, 0).wait()
        fetch(j, 1).wait()
        store(j).start()

    @pl.loop(0, slots)
    def _(j):
        store(j).wait()


def finish(place_a, place_b, partial, route_own, roll_a, roll_b):
    vmem = pl.BlockSpec(memory_space=pltpu.VMEM)
    smem = pl.BlockSpec(memory_space=pltpu.SMEM)
    anywhere = pl.BlockSpec(memory_space=pl.ANY)
    columns = roll_a.shape[-1]
    slots = place_a.shape[0]
    flat = (4 * 8 * CAP, HALF, columns)
    return pl.pallas_call(
        finish_kernel,
        out_shape=(
            jax.ShapeDtypeStruct((TOK_DEV, FCOL), jnp.bfloat16),
            jax.ShapeDtypeStruct((slots, 2 * HALF, columns), jnp.bfloat16),
        ),
        in_specs=[smem, smem, vmem, vmem, anywhere, anywhere],
        out_specs=(vmem, anywhere),
        scratch_shapes=[
            pltpu.VMEM((slots, 2 * HALF, columns), jnp.bfloat16),
            pltpu.SemaphoreType.DMA((2 * slots,)),
            pltpu.SemaphoreType.DMA((slots,)),
        ],
        compiler_params=pltpu.CompilerParams(vmem_limit_bytes=16 * 2**20),
        name="finish",
    )(place_a, place_b, partial, route_own, roll_a.reshape(flat), roll_b.reshape(flat))


def load_tables(plan, owner_index, blk_dev):
    table = plan.reshape(N_E, -1)
    slot_count = table.shape[1]
    source = table // blk_dev
    local = table % blk_dev
    positions = jnp.arange(slot_count, dtype=jnp.int32)
    same_source = source[:, :, None] == source[:, None, :]
    before = positions[:, None] > positions[None, :]
    rank = jnp.sum((same_source & before[None, :, :]).astype(jnp.int32), axis=2)
    key = source * CAP + rank
    wanted = jnp.arange(N_E * CAP, dtype=jnp.int32).reshape(N_E, 1, CAP, 1)
    sent = jnp.sum(jnp.where(key[None, :, None, :] == wanted, local[None, :, None, :], 0), axis=3)
    mine, my_rank = source[owner_index], rank[owner_index]
    dy = (mine // 8 - owner_index // 8) % 4
    dx = ((mine // 2) % 4 - (owner_index // 2) % 4) % 4
    dz = (mine - owner_index) % 2
    place_a = (dx * 8 + dy * 2 + dz) * CAP + my_rank
    place_b = (dy * 8 + dx * 2 + dz) * CAP + my_rank
    return sent.reshape(-1), place_a, place_b


def shards(
    master, grad, moment_one, moment_two, context, out_weight, hidden, norm_gain, route, plan
):
    gradient = grad.astype(jnp.float32)
    new_first = beta_one * moment_one + (1.0 - beta_one) * gradient
    new_second = beta_two * moment_two + (1.0 - beta_two) * gradient * gradient
    update = (
        new_first / bias_one / (jnp.sqrt(new_second / bias_two) + adam_eps) + decay_rate * master
    )
    new_master = master - learn_rate * update
    cast = new_master.astype(jnp.bfloat16)
    owner_index = lax.axis_index("expert")
    sent, place_a, place_b = load_tables(plan, owner_index, cast.shape[0])
    partial, roll_a, roll_b = step(context, out_weight, hidden, norm_gain, sent, cast)
    route_own = lax.dynamic_slice(route, (owner_index * TOK_DEV,), (TOK_DEV,)).reshape(TOK_DEV, 1)
    activation, rollout = finish(place_a, place_b, partial, route_own, roll_a, roll_b)
    return (new_master, new_first, new_second, rollout, activation)


def solution(mesh):
    return jax.shard_map(
        shards,
        mesh=mesh,
        in_specs=(
            P("expert", None, "tensor"),
            P("expert", None, "tensor"),
            P("expert", None, "tensor"),
            P("expert", None, "tensor"),
            P("expert", "tensor"),
            P("tensor", "expert"),
            P("expert", None),
            P(),
            P(),
            P(),
        ),
        out_specs=(
            P("expert", None, "tensor"),
            P("expert", None, "tensor"),
            P("expert", None, "tensor"),
            P("expert", None, "tensor"),
            P("expert", "tensor"),
        ),
        check_vma=False,
    )
```

time: 238 us -> 147 us (0.62)
  the two profiles are of different devices: /device:TPU:70 before, /device:TPU:0 now
where the time goes in v2:
time: 147 us; the launch traced here: 146 us
  Pallas kernels  130 us (88%)
  other arithmetic  9.57 us (7%)
  local copies, waits for them, and re-layouts  6.14 us (4%)
    pallas_call x1, Pallas kernels, step(): pl.pallas_call(step_kernel, out_shape=(jax.ShapeDtypeStruct((N_E, TOK_DEV...  120 us
    pallas_call x1, Pallas kernels, finish(): pl.pallas_call(finish_kernel, out_shape=(jax.ShapeDtypeStruct((TOK_DEV, F...  9.91 us
    convert_element_type x1, other arithmetic, shards(): cast = new_master.astype(jnp.bfloat16)  6 us
    unnamed x17, local copies, waits for them, and re-layouts  5.22 us

profile of v2, /device:TPU:0, one launch (start us, length us, event | category | flops | bytes accessed | tf_op | source)
XLA Modules:
  0.0 146.1 jit_solution(17358609673622638049)
XLA Ops:
  0.6 0.0 copy-start
  0.7 0.6 copy-done
  1.3 0.1 dynamic-slice_bitcast_fusion
  1.4 0.7 sign_compare_fusion
  2.1 0.1 ne.119
  2.2 0.1 copy.21.route
  2.3 0.7 broadcast_remainder_fusion
  3.0 0.1 rem.157
  3.0 0.1 div.75
  3.1 0.8 convert_reduce_fusion
  4.0 1.3 select_reduce_fusion
  5.3 0.3 copy.19
  5.6 0.3 reshape.134.table
  5.9 0.2 copy.20.ow
  6.1 0.0 copy-done.6
  6.1 0.0 copy-start.3
  6.1 0.0 copy-start.4
  6.1 0.0 copy-start.5
  6.1 6.0 %fusion.7 = (bf16[7,128,512]{2,1,0:T(8,128)(2,1)S(1)}, f32[7,128,512]{2,1,0:T(8,128)}, f32[7,128,512]{2,1,0:T(8,128)}, f32[7,128,512]{2,1,0:T(8,128)}) fusion(f32[7,128,512]{2,1,0:T(8,128)S(1)} %copy-done.6, bf16[7,128,512]{2,1,0:T(8,128)(2,1)} %param.11, f32[7,128,512]{2,1,0:T(8,128)} %param.12, f32[7,128,512]{2,1,0:T(8,128)} %param.13), kind=kLoop, calls=%fused_computation.47 | loop fusion | flops 7798784 | bytes 12845056 | tf_op jit(solution)/shard_map/convert_element_type | solution.py:496
  12.1 0.0 copy-done.3
  12.1 119.6 %step.1 = (bf16[32,16,640]{2,1,0:T(8,128)(2,1)S(1)}, bf16[4,8,2,64,512]{4,3,2,1,0:T(8,128)(2,1)}, bf16[4,8,2,64,512]{4,3,2,1,0:T(8,128)(2,1)}) custom-call(bf16[16,1024]{1,0:T(8,128)(2,1)S(1)} %copy-done.4, bf16[1024,224]{1,0:T(8,128)(2,1)S(1)} %copy.20.ow, bf16[16,7168]{1,0:T(8,128)(2,1)S(1)} %copy-done.3, f32[1,7168]{1,0:T(1,128)S(1)} %bitcast.33, ...), custom_call_target="tpu_custom_call" | custom-call | tf_op jit(solution)/shard_map/step/pallas_call | solution.py:369
  131.8 2.2 %copy-done.1 = bf16[4,8,2,64,512]{4,3,2,1,0:T(8,128)(2,1)S(1)} copy-done((bf16[4,8,2,64,512]{4,3,2,1,0:T(8,128)(2,1)S(1)}, bf16[4,8,2,64,512]{4,3,2,1,0:T(8,128)(2,1)}, u32[]{:S(2)}) %copy-start.1) | copy-done | bytes 4194328
  134.0 2.2 %copy-done.2 = bf16[4,8,2,64,512]{4,3,2,1,0:T(8,128)(2,1)S(1)} copy-done((bf16[4,8,2,64,512]{4,3,2,1,0:T(8,128)(2,1)S(1)}, bf16[4,8,2,64,512]{4,3,2,1,0:T(8,128)(2,1)}, u32[]{:S(2)}) %copy-start.2) | copy-done | bytes 4194328
  136.1 9.9 %finish.1 = (bf16[16,512]{1,0:T(8,128)(2,1)}, bf16[32,128,512]{2,1,0:T(8,128)(2,1)}) custom-call(s32[32]{0:T(128)S(1)} %bitcast_add_fusion.1.place_a, s32[32]{0:T(128)S(1)} %get-tuple-element.19.place_b, bf16[32,16,640]{2,1,0:T(8,128)(2,1)S(1)} %get-tuple-element.10.partial, s32[16,1]{1,0:T(8,128)S(1)} %copy.21.route, bf16[64,64,512]{2,1,0:T(8,128)(2,1)S(1)} %bitcast.31, ...), custom_call_target="tpu_custom_call" | custom-call | tf_op jit(solution)/shard_map/finish/pallas_call | solution.py:447
  (13 shorter events, 0.1 us)
Async XLA Ops:
  0.6 0.7 copy-start
  0.6 5.2 %copy-start.7 = (bf16[1024,224]{0,1:T(8,128)(2,1)S(1)}, bf16[1024,224]{0,1:T(8,128)(2,1)}, u32[]{:S(2)}) copy-start(bf16[1024,224]{0,1:T(8,128)(2,1)} %param.15) | copy-start | bytes 1376260
  0.7 5.4 %copy-start.6 = (f32[7,128,512]{2,1,0:T(8,128)S(1)}, f32[7,128,512]{2,1,0:T(8,128)}, u32[]{:S(2)}) copy-start(f32[7,128,512]{2,1,0:T(8,128)} %param.10) | copy-start | bytes 5505028
  6.1 6.0 %copy-start.3 = (bf16[16,7168]{1,0:T(8,128)(2,1)S(1)}, bf16[16,7168]{1,0:T(8,128)(2,1)}, u32[]{:S(2)}) copy-start(bf16[16,7168]{1,0:T(8,128)(2,1)} %hid.1) | copy-start | bytes 688132
  6.1 6.0 %copy-start.4 = (bf16[16,1024]{1,0:T(8,128)(2,1)S(1)}, bf16[16,1024]{1,0:T(8,128)(2,1)}, u32[]{:S(2)}) copy-start(bf16[16,1024]{1,0:T(8,128)(2,1)} %ctx.1) | copy-start | bytes 98308
  6.1 6.0 %copy-start.5 = (f32[7168]{0:T(1024)S(1)}, f32[7168]{0:T(1024)}, u32[]{:S(2)}) copy-start(f32[7168]{0:T(1024)} %param.17) | copy-start | bytes 86020
  131.8 2.2 %copy-start.1 = (bf16[4,8,2,64,512]{4,3,2,1,0:T(8,128)(2,1)S(1)}, bf16[4,8,2,64,512]{4,3,2,1,0:T(8,128)(2,1)}, u32[]{:S(2)}) copy-start(bf16[4,8,2,64,512]{4,3,2,1,0:T(8,128)(2,1)} %get-tuple-element.11) | copy-start | bytes 12582916
  134.0 2.2 %copy-start.2 = (bf16[4,8,2,64,512]{4,3,2,1,0:T(8,128)(2,1)S(1)}, bf16[4,8,2,64,512]{4,3,2,1,0:T(8,128)(2,1)}, u32[]{:S(2)}) copy-start(bf16[4,8,2,64,512]{4,3,2,1,0:T(8,128)(2,1)} %get-tuple-element.12) | copy-start | bytes 12582916

commit v3 on v2

v3 whole, which is shorter than its diff:
```python
import functools

import jax
import jax.numpy as jnp
from jax import lax
from jax.experimental import pallas as pl
from jax.experimental.pallas import tpu as pltpu
from jax.sharding import PartitionSpec as P

MESH = pl.DeviceIdType.MESH
CAP = 2
N_E = 32
N_T = 4
TOK_DEV = 16
COLS = 224
WIDE = 256
GROUP = 128
FCOL = 512
MSG = 640
HALF = 64

beta_one = 0.9
beta_two = 0.95
bias_one = 1.0 - 0.9**50
bias_two = 1.0 - 0.95**50
learn_rate = 0.0003
decay_rate = 0.1
adam_eps = 1e-08


def split_sum(total):
    high = total.astype(jnp.bfloat16)
    low = (total - high.astype(jnp.float32)).astype(jnp.bfloat16)
    return high.astype(jnp.float32), low.astype(jnp.float32)


def parts_of(wide, narrow):
    parts = [(0, True, 0, wide), (1, True, wide, wide)]
    if narrow:
        parts += [(0, False, 2 * wide, narrow), (1, False, 2 * wide + narrow, narrow)]
    return parts


PARTS = parts_of(48, 16)


def step_kernel(
    master, grad, first, second, ctx, ow_in, hid_in, gain_in, plan,
    pre_out, roll, new_master, new_first, new_second,
    table, cast, state_in, grad_in, state_out, sent_index, s_state, s_grad, s_out, s_table,
    ow, hid, gain, s_load, ctx_all,
    ow_wide, hid_send, hid_recv, gain_all, part_send, part_recv, part_own, msg, held, pre_send,
    s_ctx, r_ctx, s_row, r_row, s_hid, r_hid, s_part, r_part, s_msg, r_msg, s_held, r_held, s_pre, r_pre, local_sem,
    s_near, r_near, s_pick, r_pick, *rest
):
    picked = rest[: len(PARTS)]
    near = []
    used = len(PARTS)
    for _, z_first, _, _ in PARTS:
        count = 7 if z_first else 3
        near.append(rest[used : used + count])
        used += count
    e = lax.axis_index("expert")
    t = lax.axis_index("tensor")
    y, x, z = e // 8, (e // 2) % 4, e % 2

    loads = [
        pltpu.make_async_copy(source, target, s_load.at[i])
        for i, (source, target) in enumerate(((ow_in, ow), (hid_in, hid), (gain_in, gain)))
    ]
    for load in loads:
        load.start()

    blocks = cast.shape[0]
    arrays_in, arrays_out = (master, first, second), (new_master, new_first, new_second)

    def state_copy(b, i):
        return pltpu.make_async_copy(arrays_in[i].at[b], state_in.at[i, b], s_state.at[b * 3 + i])

    def grad_copy(b):
        return pltpu.make_async_copy(grad.at[b], grad_in.at[b], s_grad.at[b])

    @pl.loop(0, blocks)
    def _(b):
        for i in range(3):
            state_copy(b, i).start()
        grad_copy(b).start()

    barrier = pltpu.get_barrier_semaphore()

    @pl.loop(1, N_E)
    def _(i):
        pl.semaphore_signal(barrier, 1, device_id=((e + i) % N_E, t), device_id_type=MESH)

    for j in range(1, N_T):
        pl.semaphore_signal(barrier, 1, device_id=(e, (t + j) % N_T), device_id_type=MESH)
    pl.semaphore_wait(barrier, N_E - 1 + N_T - 1)

    def at(dy, dx, dz):
        return ((y + dy) % 4) * 8 + ((x + dx) % 4) * 2 + (z + dz) % 2

    def gather_to(axis, d, dz=0):
        return at(d, 0, dz) if axis == 0 else at(0, d, dz)

    def owner_at(axis, d, dz=0):
        return at(0, d, dz) if axis == 0 else at(d, 0, dz)

    def place_of(p, d, dz):
        return 2 * d + dz if PARTS[p][1] else d

    FIRST, SECOND = (0, 4), (4, 3)

    def step_of(p, step):
        if PARTS[p][1]:
            return {
                "z": (None, 1, 0, 1, None),
                "own+": (None, 6, 1, 0, None),
                "own-": (None, 2, 3, 0, None),
                "z+": (1, 7, 1, 0, None),
                "z-": (1, 3, 3, 0, None),
                "on+": (6, 4, 1, 0, None),
                "on-": (3, 5, 3, 0, None),
            }[step]
        return {
            "own+": (None, 3, 1, 0, None),
            "own-": (None, 1, 3, 0, None),
            "on+": (3, 2, 1, 0, FIRST),
            "on-": (1, 2, 3, 0, SECOND),
        }[step]

    def steps_of(p):
        return ("z", "own+", "own-", "z+", "z-", "on+", "on-") if PARTS[p][1] else ("own+", "own-", "on+", "on-")

    def near_copy(p, step):
        axis, _, row, rows = PARTS[p]
        source, place, d, dz, some = step_of(p, step)
        index = p * 8 + steps_of(p).index(step)
        if source is None:
            piece = cast.at[:, pl.ds(row, rows)]
        else:
            piece = near[p][source - 1]
        target = near[p][place - 1]
        if some is not None:
            piece, target = piece.at[pl.ds(*some)], target.at[pl.ds(*some)]
        return pltpu.make_async_remote_copy(
            piece, target, s_near.at[index], r_near.at[index],
            device_id=(gather_to(axis, d, dz), t), device_id_type=MESH,
        )

    def near_start(*steps):
        for p in range(len(PARTS)):
            for step in steps:
                if step in steps_of(p):
                    near_copy(p, step).start()

    def targets(p):
        return [(d, dz) for dz in ((0,) if PARTS[p][1] else (1, 0)) for d in (1, 3, 2, 0)]

    def pick_copy(p, d, dz, od, odz):
        axis, z_first, row, rows = PARTS[p]
        place = place_of(p, d, dz)
        index = p * 32 + place * len(targets(p)) + targets(p).index((od, odz))
        back = (4 - od) % 4
        slot = roll.at[(back, d, dz + odz) if axis == 0 else (d, back, dz + odz)]
        source, target = picked[p].at[index - p * 32], slot.at[:, pl.ds(row, rows)]
        if (od, odz) == (0, 0):
            return pltpu.make_async_copy(source, target, s_pick.at[index])
        return pltpu.make_async_remote_copy(
            source, target, s_pick.at[index], r_pick.at[index],
            device_id=(owner_at(axis, od, odz), t), device_id_type=MESH,
        )

    def pick(p, d, dz=0):
        axis, _, row, rows = PARTS[p]
        place = place_of(p, d, dz)
        source = gather_to(axis, d, dz)
        for i, (od, odz) in enumerate(targets(p)):
            owner = owner_at(axis, od, odz)
            for r in range(CAP):
                block = table[(owner % 4) * 8 + owner // 4, source * CAP + r]
                if place == 0:
                    found = cast[block, pl.ds(row, rows)]
                else:
                    found = near[p][place - 1][block]
                picked[p][place * len(targets(p)) + i, r] = found
            pick_copy(p, d, dz, od, odz).start()

    def rollout_end():
        for p in range(len(PARTS)):
            for step in steps_of(p):
                near_copy(p, step).wait_send()
            for d in range(4):
                for dz in (0, 1) if PARTS[p][1] else (0,):
                    for od, odz in targets(p):
                        pick_copy(p, d, dz, od, odz).wait()

    def out_copy(b, i):
        return pltpu.make_async_copy(state_out.at[i, b], arrays_out[i].at[b], s_out.at[b * 3 + i])

    def optimize():
        @pl.loop(0, blocks)
        def _(b):
            for i in range(3):
                state_copy(b, i).wait()
            grad_copy(b).wait()

            @pl.loop(0, cast.shape[1] // 16)
            def _(row):
                rows = pl.ds(pl.multiple_of(row * 16, 16), 16)
                weight = state_in[0, b, rows]
                gradient = grad_in[b, rows].astype(jnp.float32)
                one = beta_one * state_in[1, b, rows] + (1.0 - beta_one) * gradient
                two = beta_two * state_in[2, b, rows] + (1.0 - beta_two) * gradient * gradient
                update = (one * (1.0 / bias_one)) / (jnp.sqrt(two * (1.0 / bias_two)) + adam_eps) + decay_rate * weight
                weight = weight - learn_rate * update
                state_out[0, b, rows] = weight
                state_out[1, b, rows] = one
                state_out[2, b, rows] = two
                cast[b, rows] = weight.astype(jnp.bfloat16)

            for i in range(3):
                out_copy(b, i).start()

    def optimize_end():
        @pl.loop(0, blocks)
        def _(b):
            for i in range(3):
                out_copy(b, i).wait()

    table_copy = pltpu.make_async_copy(sent_index, table, s_table)

    def make_table():
        wanted = plan[...]
        source = (wanted * 9363) >> 16
        local = wanted - source * blocks
        lane = lax.broadcasted_iota(jnp.int32, wanted.shape, 1)
        slot = lane % N_E
        rank = jnp.zeros_like(wanted)
        for j in range(1, N_E):
            rank = rank + jnp.where((pltpu.roll(source, j, 1) == source) & (slot >= j), 1, 0)
        key = source * CAP + rank
        for quarter in range(4):
            found = jnp.zeros_like(wanted)
            for j in range(N_E):
                at_lane = quarter * N_E + j
                found = found + jnp.where(key[:, at_lane : at_lane + 1] == lane, local[:, at_lane : at_lane + 1], 0)
            sent_index[pl.ds(quarter * 8, 8)] = found
        table_copy.start()
        table_copy.wait()

    width = ctx_all.shape[-1]

    def ctx_copy(half, i):
        target = gather_to(half, i // 2, i % 2)
        return pltpu.make_async_remote_copy(
            ctx.at[:, pl.ds(half * width, width)], ctx_all.at[half, y, x, z], s_ctx.at[half * 8 + i], r_ctx.at[half * 8 + i],
            device_id=(target, t), device_id_type=MESH,
        )

    def row_copy(half, d):
        rows = ctx_all.at[0, :, x] if half == 0 else ctx_all.at[1, y]
        return pltpu.make_async_remote_copy(
            rows, rows, s_row.at[half * 4 + d], r_row.at[half * 4 + d],
            device_id=(owner_at(half, d), t), device_id_type=MESH,
        )

    def ctx_own(half):
        return pltpu.make_async_copy(
            ctx.at[:, pl.ds(half * width, width)], ctx_all.at[half, y, x, z], s_ctx.at[half * 8]
        )

    def ctx_start():
        for half in (0, 1):
            for i in range(1, 8):
                ctx_copy(half, i).start()
            ctx_own(half).start()

    def row_start():
        for half in (0, 1):
            ctx_own(half).wait()
            for i in range(1, 8):
                ctx_copy(half, i).wait_recv()
            for d in (1, 3, 2):
                row_copy(half, d).start()

    spot = x * 2 + z
    sends_hidden = y == t

    def hid_copy(i):
        return pltpu.make_async_remote_copy(
            hid_send.at[(e + i) % N_E], hid_recv.at[spot], s_hid.at[i], r_hid.at[spot],
            device_id=((e + i) % N_E, t), device_id_type=MESH,
        )

    def hid_start():
        loads[1].wait()

        @pl.when(sends_hidden)
        def _():
            hid_send[...] = jnp.zeros_like(hid_send)
            for g in range(N_E):
                hid_send[g, :, :COLS] = hid[:, g * COLS : (g + 1) * COLS]

            @pl.loop(1, N_E)
            def _(i):
                hid_copy(i).start()

            hid_recv[spot] = hid_send[e]

    def prepare():
        loads[0].wait()
        loads[2].wait()
        gain_all[...] = jnp.zeros_like(gain_all)
        for g in range(N_E):
            gain_all[g, :, :COLS] = gain[:, g * COLS : (g + 1) * COLS]
        ow_wide[...] = jnp.zeros_like(ow_wide)
        ow_wide[:COLS] = ow[...]

    def ctx_wait():
        for half in (0, 1):
            for d in (1, 2, 3):
                row_copy(half, d).wait_recv()

    def projected(group):
        total = jnp.zeros((GROUP, WIDE), jnp.float32)
        for half in (0, 1):
            values = ctx_all[half, group].reshape(GROUP, width)
            weight = ow_wide[:, half * width : (half + 1) * width]
            total = total + lax.dot_general(
                values, weight, (((1,), (1,)), ((), ())), preferred_element_type=jnp.float32
            )
        return total

    def part_copy(j):
        return pltpu.make_async_remote_copy(
            part_send.at[j], part_recv.at[j], s_part.at[j], r_part.at[j],
            device_id=(e, (t + j) % N_T), device_id_type=MESH,
        )

    def project():
        for j in (2, 3, 1):
            part_send[j] = projected((t + j) % N_T).astype(jnp.bfloat16)
            part_copy(j).start()
        part_own[...] = projected(t)

    def residual():
        for q in range(8):
            @pl.when(t * 8 + q != e)
            def _(q=q):
                pltpu.make_async_copy(hid_recv.at[q], hid_recv.at[q], r_hid.at[q]).wait()

        resid = part_own[...] + hid_recv[...].reshape(GROUP, WIDE).astype(jnp.float32)
        for j in (1, 2, 3):
            part_copy(j).wait_recv()
            resid = resid + part_recv[j].astype(jnp.float32)
        high, low = split_sum(jnp.sum(resid * resid, axis=1, keepdims=True))
        lane = lax.broadcasted_iota(jnp.int32, (GROUP, WIDE), 1)
        scaled = resid * gain_all[e]
        scaled = jnp.where(lane == COLS, high, jnp.where(lane == COLS + 1, low, scaled))
        msg[...] = scaled.astype(jnp.bfloat16)

    spot_in = (x % 2) * 2 + z
    my_slice = 2 * x + z

    def msg_copy(k):
        target = k * 8 + 2 * y + x // 2
        return target, pltpu.make_async_remote_copy(
            msg, held.at[t, spot_in], s_msg.at[k], r_msg.at[spot_in], device_id=(target, t), device_id_type=MESH
        )

    def msg_start():
        for k in range(4):
            target, copy = msg_copy(k)

            @pl.when(target != e)
            def _(copy=copy):
                copy.start()

            @pl.when(target == e)
            def _():
                held[t, spot_in] = msg[...]

    def msg_wait():
        for j in range(4):
            @pl.when(my_slice * 4 + j != e)
            def _(j=j):
                pltpu.make_async_copy(held.at[t, j], held.at[t, j], r_msg.at[j]).wait()

    def held_copy(j):
        return pltpu.make_async_remote_copy(
            held.at[t], held.at[t], s_held.at[j], r_held.at[j], device_id=(e, (t + j) % N_T), device_id_type=MESH
        )

    def held_start():
        for j in (2, 3, 1):
            held_copy(j).start()

    def pre_copy(o):
        return pltpu.make_async_remote_copy(
            pre_send.at[o], pre_out.at[e], s_pre.at[o], r_pre.at[e], device_id=(o, t), device_id_type=MESH
        )

    own_copy = pltpu.make_async_copy(pre_send.at[e], pre_out.at[e], local_sem)

    tail_lane = lax.broadcasted_iota(jnp.int32, (GROUP, MSG - FCOL), 1)

    def expert_rows(j):
        if j:
            group = (t + N_T - j) % N_T
            pltpu.make_async_copy(held.at[group], held.at[group], r_held.at[j]).wait()
        else:
            group = t
        weight = cast[...].reshape(896, FCOL)
        total = jnp.zeros((GROUP, FCOL), jnp.float32)
        squares = jnp.zeros((GROUP, 1), jnp.float32)
        for i in range(4):
            block = held[group, i]
            total = total + jnp.dot(
                block[:, :COLS], weight[i * COLS : (i + 1) * COLS], preferred_element_type=jnp.float32
            )
            tail = block[:, GROUP:].astype(jnp.float32)
            squares = squares + jnp.sum(
                jnp.where(tail_lane >= COLS - GROUP, tail, 0.0), axis=1, keepdims=True
            )
        high, low = split_sum(squares)
        extra = jnp.where(tail_lane == 0, high, jnp.where(tail_lane == 1, low, 0.0))
        pre_send[pl.ds(group * 8, 8), :, :FCOL] = total.astype(jnp.bfloat16).reshape(8, TOK_DEV, FCOL)
        pre_send[pl.ds(group * 8, 8), :, FCOL:] = extra.astype(jnp.bfloat16).reshape(8, TOK_DEV, MSG - FCOL)

        @pl.loop(0, 8)
        def _(q, group=group):
            o = group * 8 + q

            @pl.when(o != e)
            def _():
                pre_copy(o).start()

            @pl.when(o == e)
            def _():
                own_copy.start()

    def finish_decode():
        own_copy.wait()

        @pl.loop(1, N_E)
        def _(i):
            source = (e + i) % N_E
            pltpu.make_async_copy(pre_send.at[source], pre_out.at[source], r_pre.at[source]).wait()
            pre_copy(source).wait_send()

        @pl.when(sends_hidden)
        def _():
            @pl.loop(1, N_E)
            def _(i):
                hid_copy(i).wait_send()

        for half in (0, 1):
            for i in range(1, 8):
                ctx_copy(half, i).wait_send()
            for d in (1, 2, 3):
                row_copy(half, d).wait_send()
        for j in (1, 2, 3):
            part_copy(j).wait_send()
            held_copy(j).wait_send()
        for k in range(4):
            target, copy = msg_copy(k)

            @pl.when(target != e)
            def _(copy=copy):
                copy.wait_send()

    n_parts = range(len(PARTS))
    z_parts = [p for p in n_parts if PARTS[p][1]]
    flat_parts = [p for p in n_parts if not PARTS[p][1]]
    ctx_start()
    optimize()
    row_start()
    near_start("z")
    near_start("own+", "own-")
    make_table()
    prepare()
    hid_start()
    for p in z_parts:
        pick(p, 0)
    ctx_wait()
    project()
    for p in flat_parts:
        pick(p, 0)
    for p in z_parts:
        near_copy(p, "z").wait_recv()
        near_copy(p, "z+").start()
        near_copy(p, "z-").start()
    residual()
    msg_start()
    for p in n_parts:
        near_copy(p, "own+").wait_recv()
        near_copy(p, "on+").start()
    for p in flat_parts:
        near_copy(p, "own-").wait_recv()
        near_copy(p, "on-").start()
    for p in z_parts:
        pick(p, 0, 1)
    msg_wait()
    held_start()
    for p in z_parts:
        near_copy(p, "z-").wait_recv()
        near_copy(p, "on-").start()
    for p in z_parts:
        pick(p, 3)
    for p in z_parts:
        near_copy(p, "own-").wait_recv()
        pick(p, 1)
    expert_rows(0)
    expert_rows(1)
    expert_rows(2)
    expert_rows(3)
    for p in flat_parts:
        pick(p, 1)
        pick(p, 3)
    for p in z_parts:
        pick(p, 1, 1)
    for p in z_parts:
        near_copy(p, "z+").wait_recv()
        pick(p, 3, 1)
    for p in flat_parts:
        near_copy(p, "on+").wait_recv()
        near_copy(p, "on-").wait_recv()
        pick(p, 2)
    for p in z_parts:
        near_copy(p, "on+").wait_recv()
        pick(p, 2)
    for p in z_parts:
        near_copy(p, "on-").wait_recv()
        pick(p, 2, 1)

    optimize_end()
    finish_decode()
    rollout_end()


def step(master, grad, first, second, context, out_weight, hidden, norm_gain, plan):
    vmem = pl.BlockSpec(memory_space=pltpu.VMEM)
    anywhere = pl.BlockSpec(memory_space=pl.ANY)
    dma = pltpu.SemaphoreType.DMA
    bf16 = jnp.bfloat16
    blocks, block_rows, columns = master.shape
    state = jax.ShapeDtypeStruct(master.shape, jnp.float32)
    depth = out_weight.shape[0]
    width = hidden.shape[1]
    return pl.pallas_call(
        step_kernel,
        out_shape=(
            jax.ShapeDtypeStruct((N_E, TOK_DEV, MSG), bf16),
            jax.ShapeDtypeStruct((4, 4, 2, CAP, block_rows, columns), bf16),
            state, state, state,
        ),
        in_specs=[anywhere] * 8 + [vmem],
        out_specs=(anywhere,) * 5,
        scratch_shapes=[
            pltpu.SMEM((N_E, 128), jnp.int32),
            pltpu.VMEM(master.shape, bf16),
            pltpu.VMEM((3, *master.shape), jnp.float32),
            pltpu.VMEM(master.shape, bf16),
            pltpu.VMEM((3, *master.shape), jnp.float32),
            pltpu.VMEM((N_E, 128), jnp.int32),
            dma((3 * blocks,)), dma((blocks,)), dma((3 * blocks,)), dma,
            pltpu.VMEM((COLS, depth), bf16),
            pltpu.VMEM((TOK_DEV, width), bf16),
            pltpu.VMEM((1, width), jnp.float32),
            dma((3,)),
            pltpu.VMEM((2, 4, 4, 2, TOK_DEV, depth // 2), bf16),
            pltpu.VMEM((WIDE, depth), bf16),
            pltpu.VMEM((N_E, TOK_DEV, WIDE), bf16),
            pltpu.VMEM((8, TOK_DEV, WIDE), bf16),
            pltpu.VMEM((N_E, 1, WIDE), jnp.float32),
            pltpu.VMEM((N_T, GROUP, WIDE), bf16),
            pltpu.VMEM((N_T, GROUP, WIDE), bf16),
            pltpu.VMEM((GROUP, WIDE), jnp.float32),
            pltpu.VMEM((GROUP, WIDE), bf16),
            pltpu.VMEM((N_T, 4, GROUP, WIDE), bf16),
            pltpu.VMEM((N_E, TOK_DEV, MSG), bf16),
            dma((16,)), dma((16,)), dma((8,)), dma((8,)),
            dma((N_E,)), dma((8,)), dma((N_T,)), dma((N_T,)), dma((4,)), dma((4,)),
            dma((N_T,)), dma((N_T,)), dma((N_E,)), dma((N_E,)), dma,
            dma((32,)), dma((32,)), dma((128,)), dma((128,)),
            *[pltpu.VMEM((32, CAP, rows, columns), bf16) for _, _, _, rows in PARTS],
            *[
                pltpu.VMEM((blocks, rows, columns), bf16)
                for _, z_first, _, rows in PARTS
                for _ in range(7 if z_first else 3)
            ],
        ],
        compiler_params=pltpu.CompilerParams(
            collective_id=0, has_side_effects=True, vmem_limit_bytes=56 * 2**20
        ),
        name="step",
    )(
        master, grad, first, second, context, out_weight.T, hidden, norm_gain.reshape(1, -1), plan.reshape(8, 128)
    )


def finish_kernel(
    plan, route, partial_in, roll, master_in, first_in, second_in,
    out, rollout, master, first, second,
    stage, state, partial, seen, in_sems, out_sems, state_in_sems, state_out_sems, partial_sem,
):
    e = lax.axis_index("expert")
    slots = rollout.shape[0]
    sources, targets = (master_in, first_in, second_in), (master, first, second)

    def fetch(j, place):
        return pltpu.make_async_copy(roll.at[place], stage.at[j], in_sems.at[j])

    def store(j):
        return pltpu.make_async_copy(stage.at[j], rollout.at[j], out_sems.at[j])

    def state_in(i):
        return pltpu.make_async_copy(sources[i], state.at[i], state_in_sems.at[i])

    def state_out(i):
        return pltpu.make_async_copy(state.at[i], targets[i], state_out_sems.at[i])

    partial_copy = pltpu.make_async_copy(partial_in, partial, partial_sem)
    partial_copy.start()
    for i in range(3):
        state_in(i).start()

    @pl.loop(0, N_E)
    def _(j):
        seen[j] = 0

    @pl.loop(0, slots)
    def _(j):
        source = (plan[e * slots + j] * 9363) >> 16
        rank = seen[source]
        seen[source] = rank + 1
        dy = (source // 8 + 4 - e // 8) % 4
        dx = (source // 2 + 4 - (e // 2) % 4) % 4
        dz = (source + e) % 2
        fetch(j, ((dx * 4 + dy) * 2 + dz) * CAP + rank).start()

    for i in range(3):
        state_in(i).wait()
        state_out(i).start()

    @pl.loop(0, slots)
    def _(j):
        fetch(j, 0).wait()
        store(j).start()

    partial_copy.wait()
    token = lax.broadcasted_iota(jnp.int32, (TOK_DEV, 1), 0)
    expert = jnp.zeros((TOK_DEV, 1), jnp.int32)
    for i in range(TOK_DEV):
        expert = jnp.where(token == i, route[e * TOK_DEV + i], expert)
    pre = jnp.zeros((TOK_DEV, FCOL), jnp.float32)
    squares = jnp.zeros((TOK_DEV, 1), jnp.float32)
    for k in range(4):
        total = jnp.zeros((TOK_DEV, FCOL), jnp.float32)
        for h in range(8):
            total = total + partial[k * 8 + h, :, :FCOL].astype(jnp.float32)
        pre = pre + jnp.where(expert == k, total, 0.0)
    for h in range(8):
        squares = squares + jnp.sum(partial[h, :, FCOL:].astype(jnp.float32), axis=1, keepdims=True)
    pre = pre * lax.rsqrt(squares / (N_E * COLS) + 1e-06)
    out[...] = (pre / (1.0 + jnp.exp(-pre))).astype(jnp.bfloat16)

    @pl.loop(0, slots)
    def _(j):
        store(j).wait()

    for i in range(3):
        state_out(i).wait()


def finish(plan, route, partial, roll, state):
    vmem = pl.BlockSpec(memory_space=pltpu.VMEM)
    smem = pl.BlockSpec(memory_space=pltpu.SMEM)
    anywhere = pl.BlockSpec(memory_space=pl.ANY)
    block_rows, columns = roll.shape[-2:]
    slots = plan.shape[0] // N_E
    shape = jax.ShapeDtypeStruct(state[0].shape, jnp.float32)
    dma = pltpu.SemaphoreType.DMA
    return pl.pallas_call(
        finish_kernel,
        out_shape=(
            jax.ShapeDtypeStruct((TOK_DEV, FCOL), jnp.bfloat16),
            jax.ShapeDtypeStruct((slots, block_rows, columns), jnp.bfloat16),
            shape, shape, shape,
        ),
        in_specs=[smem, smem] + [anywhere] * 5,
        out_specs=(vmem,) + (anywhere,) * 4,
        scratch_shapes=[
            pltpu.VMEM((slots, block_rows, columns), jnp.bfloat16),
            pltpu.VMEM((3, *state[0].shape), jnp.float32),
            pltpu.VMEM(partial.shape, partial.dtype),
            pltpu.SMEM((N_E,), jnp.int32),
            dma((slots,)), dma((slots,)), dma((3,)), dma((3,)), dma,
        ],
        compiler_params=pltpu.CompilerParams(vmem_limit_bytes=56 * 2**20),
        name="finish",
    )(plan, route, partial, roll.reshape(4 * 4 * 2 * CAP, block_rows, columns), *state)


def shards(
    master, grad, moment_one, moment_two, context, out_weight, hidden, norm_gain, route, plan
):
    partial, roll, *state = step(
        master, grad, moment_one, moment_two, context, out_weight, hidden, norm_gain, plan
    )
    activation, rollout, *state = finish(plan, route, partial, roll, state)
    return (*state, rollout, activation)


def solution(mesh):
    return jax.shard_map(
        shards,
        mesh=mesh,
        in_specs=(
            P("expert", None, "tensor"),
            P("expert", None, "tensor"),
            P("expert", None, "tensor"),
            P("expert", None, "tensor"),
            P("expert", "tensor"),
            P("tensor", "expert"),
            P("expert", None),
            P(),
            P(),
            P(),
        ),
        out_specs=(
            P("expert", None, "tensor"),
            P("expert", None, "tensor"),
            P("expert", None, "tensor"),
            P("expert", None, "tensor"),
            P("expert", "tensor"),
        ),
        check_vma=False,
    )
```

time: 147 us -> 127 us (0.86)
  other arithmetic: 9.57 us -> 0 us
  local copies, waits for them, and re-layouts: 6.14 us -> 0 us
  Pallas kernels: 130 us -> 126 us
    convert_element_type x1 -> x0, other arithmetic: 6 us -> none  [shards(): cast = new_master.astype(jnp.bfloat16)]
    unnamed x17 -> x0, local copies, waits for them, and re-layouts: 5.22 us -> none
    pallas_call x1, Pallas kernels: 120 us -> 116 us  [step(): pl.pallas_call(step_kernel, out_shape=(jax.ShapeDtypeStruct((N_E, TOK_DEV...]
    reduce_sum x2 -> x0, other arithmetic: 2.09 us -> none  [the longest x1 1.31 us: load_tables(): jnp.sum(jnp.where(key[None, :, None, :] == wanted, local[None, :, None, :...]
where the time goes in v3:
time: 127 us
  Pallas kernels  126 us (99%)
    pallas_call x1, Pallas kernels, step(): pl.pallas_call(step_kernel, out_shape=(jax.ShapeDtypeStruct((N_E, TOK_DEV...  116 us
    pallas_call x1, Pallas kernels, finish(): pl.pallas_call(finish_kernel, out_shape=(jax.ShapeDtypeStruct((TOK_DEV, F...  9.73 us

profile of v3, /device:TPU:0, one launch (start us, length us, event | category | flops | bytes accessed | tf_op | source)
XLA Modules:
  0.0 126.7 jit_solution(5207499120623401091)
XLA Ops:
  0.6 116.3 %step.1 = (bf16[32,16,640]{2,1,0:T(8,128)(2,1)}, bf16[4,4,2,2,128,512]{5,4,3,2,1,0:T(8,128)(2,1)}, f32[7,128,512]{2,1,0:T(8,128)}, f32[7,128,512]{2,1,0:T(8,128)}, f32[7,128,512]{2,1,0:T(8,128)}) custom-call(f32[7,128,512]{2,1,0:T(8,128)} %master.1, bf16[7,128,512]{2,1,0:T(8,128)(2,1)} %grad.1, f32[7,128,512]{2,1,0:T(8,128)} %first.1, ...), custom_call_target="tpu_custom_call" | custom-call | tf_op jit(solution)/shard_map/step/pallas_call | solution.py:550
  116.9 9.7 %finish.1 = (bf16[16,512]{1,0:T(8,128)(2,1)}, bf16[32,128,512]{2,1,0:T(8,128)(2,1)}, f32[7,128,512]{2,1,0:T(8,128)}, f32[7,128,512]{2,1,0:T(8,128)}, f32[7,128,512]{2,1,0:T(8,128)}) custom-call(s32[1024]{0:T(1024)} %plan.1, s32[512]{0:T(512)} %route.1, bf16[32,16,640]{2,1,0:T(8,128)(2,1)} %get-tuple-element.15.partial_in, bf16[64,128,512]{2,1,0:T(8,128)(2,1)} %bitcast.4, ...), custom_call_target="tpu_custom_call" | custom-call | tf_op jit(solution)/shard_map/finish/pallas_call | solution.py:684

commit v4 on v3

--- a/solution.py
+++ b/solution.py
@@ -16,7 +16,6 @@
 WIDE = 256
 GROUP = 128
 FCOL = 512
-MSG = 640
 HALF = 64
 
 beta_one = 0.9
@@ -42,16 +41,17 @@
 
 
 PARTS = parts_of(48, 16)
+EARLY = 2
 
 
 def step_kernel(
     master, grad, first, second, ctx, ow_in, hid_in, gain_in, plan,
-    pre_out, roll, new_master, new_first, new_second,
+    pre_out, square_out, roll, new_master, new_first, new_second,
     table, cast, state_in, grad_in, state_out, sent_index, s_state, s_grad, s_out, s_table,
     ow, hid, gain, s_load, ctx_all,
-    ow_wide, hid_send, hid_recv, gain_all, part_send, part_recv, part_own, msg, held, pre_send,
-    s_ctx, r_ctx, s_row, r_row, s_hid, r_hid, s_part, r_part, s_msg, r_msg, s_held, r_held, s_pre, r_pre, local_sem,
-    s_near, r_near, s_pick, r_pick, *rest
+    ow_wide, hid_send, hid_recv, gain_all, part_send, part_recv, part_own, msg, held, pre_send, pair_recv, pair_sum, s_pair, r_pair,
+    s_ctx, r_ctx, s_row, r_row, s_hid, r_hid, s_part, r_part, s_lift, r_lift, s_msg, r_msg, s_held, r_held, s_pre, r_pre, local_sem,
+    square_send, s_square, r_square, s_near, r_near, s_pick, r_pick, *rest
 ):
     picked = rest[: len(PARTS)]
     near = []
@@ -109,39 +109,42 @@
         return 2 * d + dz if PARTS[p][1] else d
 
     FIRST, SECOND = (0, 4), (4, 3)
+    HEAD, TAIL = (0, EARLY), (EARLY, blocks - EARLY)
 
     def step_of(p, step):
         if PARTS[p][1]:
             return {
-                "z": (None, 1, 0, 1, None),
-                "own+": (None, 6, 1, 0, None),
-                "own-": (None, 2, 3, 0, None),
+                "z": (None, 1, 0, 1, HEAD),
+                "own+": (None, 6, 1, 0, HEAD),
+                "own-": (None, 2, 3, 0, HEAD),
+                "z b": (None, 1, 0, 1, TAIL),
+                "own+ b": (None, 6, 1, 0, TAIL),
+                "own- b": (None, 2, 3, 0, TAIL),
                 "z+": (1, 7, 1, 0, None),
                 "z-": (1, 3, 3, 0, None),
                 "on+": (6, 4, 1, 0, None),
                 "on-": (3, 5, 3, 0, None),
             }[step]
         return {
-            "own+": (None, 3, 1, 0, None),
-            "own-": (None, 1, 3, 0, None),
+            "own+": (None, 3, 1, 0, HEAD),
+            "own-": (None, 1, 3, 0, HEAD),
+            "own+ b": (None, 3, 1, 0, TAIL),
+            "own- b": (None, 1, 3, 0, TAIL),
             "on+": (3, 2, 1, 0, FIRST),
             "on-": (1, 2, 3, 0, SECOND),
         }[step]
 
     def steps_of(p):
-        return ("z", "own+", "own-", "z+", "z-", "on+", "on-") if PARTS[p][1] else ("own+", "own-", "on+", "on-")
+        shared = ("own+", "own-", "own+ b", "own- b", "on+", "on-")
+        return (*shared, "z", "z b", "z+", "z-") if PARTS[p][1] else shared
 
     def near_copy(p, step):
         axis, _, row, rows = PARTS[p]
         source, place, d, dz, some = step_of(p, step)
-        index = p * 8 + steps_of(p).index(step)
-        if source is None:
-            piece = cast.at[:, pl.ds(row, rows)]
-        else:
-            piece = near[p][source - 1]
-        target = near[p][place - 1]
-        if some is not None:
-            piece, target = piece.at[pl.ds(*some)], target.at[pl.ds(*some)]
+        index = p * 10 + steps_of(p).index(step)
+        some = pl.ds(*(some or (0, blocks)))
+        piece = cast.at[some, pl.ds(row, rows)] if source is None else near[p][source - 1].at[some]
+        target = near[p][place - 1].at[some]
         return pltpu.make_async_remote_copy(
             piece, target, s_near.at[index], r_near.at[index],
             device_id=(gather_to(axis, d, dz), t), device_id_type=MESH,
@@ -152,6 +155,11 @@
             for step in steps:
                 if step in steps_of(p):
                     near_copy(p, step).start()
+
+    def near_wait(p, step):
+        near_copy(p, step).wait_recv()
+        if step + " b" in steps_of(p):
+            near_copy(p, step + " b").wait_recv()
 
     def targets(p):
         return [(d, dz) for dz in ((0,) if PARTS[p][1] else (1, 0)) for d in (1, 3, 2, 0)]
@@ -197,16 +205,16 @@
     def out_copy(b, i):
         return pltpu.make_async_copy(state_out.at[i, b], arrays_out[i].at[b], s_out.at[b * 3 + i])
 
-    def optimize():
-        @pl.loop(0, blocks)
+    def optimize(start, count):
+        @pl.loop(start, start + count)
         def _(b):
             for i in range(3):
                 state_copy(b, i).wait()
             grad_copy(b).wait()
 
-            @pl.loop(0, cast.shape[1] // 16)
+            @pl.loop(0, cast.shape[1] // 32)
             def _(row):
-                rows = pl.ds(pl.multiple_of(row * 16, 16), 16)
+                rows = pl.ds(pl.multiple_of(row * 32, 32), 32)
                 weight = state_in[0, b, rows]
                 gradient = grad_in[b, rows].astype(jnp.float32)
                 one = beta_one * state_in[1, b, rows] + (1.0 - beta_one) * gradient
@@ -264,6 +272,15 @@
             device_id=(owner_at(half, d), t), device_id_type=MESH,
         )
 
+    def relay_copy(half, d):
+        some = pl.ds(0 if d == 1 else 2, 2)
+        rows = ctx_all.at[0, some, (x + 4 - d) % 4] if half == 0 else ctx_all.at[1, (y + 4 - d) % 4, some]
+        index = half * 4 + d - 1
+        return pltpu.make_async_remote_copy(
+            rows, rows, s_row.at[index], r_row.at[index],
+            device_id=(owner_at(half, d), t), device_id_type=MESH,
+        )
+
     def ctx_own(half):
         return pltpu.make_async_copy(
             ctx.at[:, pl.ds(half * width, width)], ctx_all.at[half, y, x, z], s_ctx.at[half * 8]
@@ -280,8 +297,14 @@
             ctx_own(half).wait()
             for i in range(1, 8):
                 ctx_copy(half, i).wait_recv()
-            for d in (1, 3, 2):
+            for d in (1, 3):
                 row_copy(half, d).start()
+
+    def row_on():
+        for half in (0, 1):
+            for d in (1, 3):
+                row_copy(half, d).wait_recv()
+                relay_copy(half, d).start()
 
     spot = x * 2 + z
     sends_hidden = y == t
@@ -318,8 +341,8 @@
 
     def ctx_wait():
         for half in (0, 1):
-            for d in (1, 2, 3):
-                row_copy(half, d).wait_recv()
+            for d in (1, 3):
+                relay_copy(half, d).wait_recv()
 
     def projected(group):
         total = jnp.zeros((GROUP, WIDE), jnp.float32)
@@ -357,95 +380,156 @@
         lane = lax.broadcasted_iota(jnp.int32, (GROUP, WIDE), 1)
         scaled = resid * gain_all[e]
         scaled = jnp.where(lane == COLS, high, jnp.where(lane == COLS + 1, low, scaled))
-        msg[...] = scaled.astype(jnp.bfloat16)
+        msg[y] = scaled.astype(jnp.bfloat16)
 
     spot_in = (x % 2) * 2 + z
-    my_slice = 2 * x + z
-
-    def msg_copy(k):
-        target = k * 8 + 2 * y + x // 2
+
+    def lift_copy(d):
+        return pltpu.make_async_remote_copy(
+            msg.at[y], msg.at[y], s_lift.at[d], r_lift.at[d], device_id=(at(d, 0, 0), t), device_id_type=MESH
+        )
+
+    def msg_copy(column):
+        target = y * 8 + column * 2 + x // 2
         return target, pltpu.make_async_remote_copy(
-            msg, held.at[t, spot_in], s_msg.at[k], r_msg.at[spot_in], device_id=(target, t), device_id_type=MESH
-        )
+            msg.at[column], held.at[t, spot_in], s_msg.at[column], r_msg.at[spot_in],
+            device_id=(target, t), device_id_type=MESH,
+        )
+
+    def msg_pass(column):
+        target, copy = msg_copy(column)
+
+        @pl.when(target != e)
+        def _():
+            copy.start()
+
+        @pl.when(target == e)
+        def _():
+            held[t, spot_in] = msg[column]
 
     def msg_start():
-        for k in range(4):
-            target, copy = msg_copy(k)
-
-            @pl.when(target != e)
-            def _(copy=copy):
-                copy.start()
-
-            @pl.when(target == e)
-            def _():
-                held[t, spot_in] = msg[...]
+        for d in (2, 1, 3):
+            lift_copy(d).start()
+        msg_pass(y)
+
+    def msg_on():
+        for d in (1, 3, 2):
+            source = (y + 4 - d) % 4
+            pltpu.make_async_copy(msg.at[source], msg.at[source], r_lift.at[d]).wait()
+            msg_pass(source)
 
     def msg_wait():
         for j in range(4):
-            @pl.when(my_slice * 4 + j != e)
+            @pl.when((x != 2 * z + j // 2) | (z != j % 2))
             def _(j=j):
                 pltpu.make_async_copy(held.at[t, j], held.at[t, j], r_msg.at[j]).wait()
 
-    def held_copy(j):
-        return pltpu.make_async_remote_copy(
-            held.at[t], held.at[t], s_held.at[j], r_held.at[j], device_id=(e, (t + j) % N_T), device_id_type=MESH
+    other_core = t + 1 - 2 * (t % 2)
+    other_chip = (t + 2) % N_T
+    far = (other_core + 2) % N_T
+
+    def held_copy(i):
+        group, target = ((t, other_chip), (t, other_core), (other_chip, other_core))[i]
+        return pltpu.make_async_remote_copy(
+            held.at[group], held.at[group], s_held.at[i], r_held.at[i], device_id=(e, target), device_id_type=MESH
         )
 
     def held_start():
-        for j in (2, 3, 1):
-            held_copy(j).start()
+        held_copy(0).start()
+        held_copy(1).start()
+
+    def held_on():
+        held_copy(0).wait_recv()
+        held_copy(2).start()
+
+    def pair_copy(group):
+        return pltpu.make_async_remote_copy(
+            pre_send.at[pl.ds(group * 4, 4), 1 - z], pair_recv.at[pl.ds(group * 4, 4)],
+            s_pair.at[group], r_pair.at[group], device_id=(at(0, 0, 1), t), device_id_type=MESH,
+        )
+
+    plane_spot = y * 4 + x
 
     def pre_copy(o):
         return pltpu.make_async_remote_copy(
-            pre_send.at[o], pre_out.at[e], s_pre.at[o], r_pre.at[e], device_id=(o, t), device_id_type=MESH
-        )
-
-    own_copy = pltpu.make_async_copy(pre_send.at[e], pre_out.at[e], local_sem)
-
-    tail_lane = lax.broadcasted_iota(jnp.int32, (GROUP, MSG - FCOL), 1)
-
-    def expert_rows(j):
-        if j:
-            group = (t + N_T - j) % N_T
-            pltpu.make_async_copy(held.at[group], held.at[group], r_held.at[j]).wait()
-        else:
-            group = t
-        weight = cast[...].reshape(896, FCOL)
+            pair_sum.at[o], pre_out.at[plane_spot], s_pre.at[o], r_pre.at[plane_spot],
+            device_id=(o * 2 + z, t), device_id_type=MESH,
+        )
+
+    own_copy = pltpu.make_async_copy(pair_sum.at[plane_spot], pre_out.at[plane_spot], local_sem.at[0])
+
+    def expert_rows(i):
+        group = (t, other_core, other_chip, far)[i]
+        if i in (1, 3):
+            pltpu.make_async_copy(held.at[group], held.at[group], r_held.at[1 if i == 1 else 2]).wait()
+        weight = cast[...].reshape(-1, FCOL)
         total = jnp.zeros((GROUP, FCOL), jnp.float32)
+        for j in range(4):
+            total = total + jnp.dot(
+                held[group, j][:, :COLS], weight[j * COLS : (j + 1) * COLS], preferred_element_type=jnp.float32
+            )
+        pre_send[pl.ds(group * 4, 4)] = total.astype(jnp.bfloat16).reshape(4, 2, TOK_DEV, FCOL)
+        pair_copy(group).start()
+
+    def expert_sums(i):
+        group = (t, other_core, other_chip, far)[i]
+        pair_copy(group).wait_recv()
+        rows = pl.ds(group * 4, 4)
+        total = pre_send[rows, z].astype(jnp.float32) + pair_recv[rows].astype(jnp.float32)
+        pair_sum[rows] = total.astype(jnp.bfloat16)
+
+        @pl.loop(0, 4)
+        def _(q):
+            o = group * 4 + q
+
+            @pl.when(o != plane_spot)
+            def _():
+                pre_copy(o).start()
+
+            @pl.when(o == plane_spot)
+            def _():
+                own_copy.start()
+
+    def square_copy(q):
+        return pltpu.make_async_remote_copy(
+            square_send.at[q], square_out.at[spot], s_square.at[q], r_square.at[spot],
+            device_id=(y * 8 + q, t), device_id_type=MESH,
+        )
+
+    own_squares = pltpu.make_async_copy(square_send.at[spot], square_out.at[spot], local_sem.at[1])
+
+    def squares_start():
+        tail_lane = lax.broadcasted_iota(jnp.int32, (GROUP, WIDE - GROUP), 1)
         squares = jnp.zeros((GROUP, 1), jnp.float32)
-        for i in range(4):
-            block = held[group, i]
-            total = total + jnp.dot(
-                block[:, :COLS], weight[i * COLS : (i + 1) * COLS], preferred_element_type=jnp.float32
-            )
-            tail = block[:, GROUP:].astype(jnp.float32)
-            squares = squares + jnp.sum(
-                jnp.where(tail_lane >= COLS - GROUP, tail, 0.0), axis=1, keepdims=True
-            )
+        for j in range(4):
+            tail = held[y, j][:, GROUP:].astype(jnp.float32)
+            squares = squares + jnp.sum(jnp.where(tail_lane >= COLS - GROUP, tail, 0.0), axis=1, keepdims=True)
         high, low = split_sum(squares)
         extra = jnp.where(tail_lane == 0, high, jnp.where(tail_lane == 1, low, 0.0))
-        pre_send[pl.ds(group * 8, 8), :, :FCOL] = total.astype(jnp.bfloat16).reshape(8, TOK_DEV, FCOL)
-        pre_send[pl.ds(group * 8, 8), :, FCOL:] = extra.astype(jnp.bfloat16).reshape(8, TOK_DEV, MSG - FCOL)
-
-        @pl.loop(0, 8)
-        def _(q, group=group):
-            o = group * 8 + q
-
-            @pl.when(o != e)
-            def _():
-                pre_copy(o).start()
-
-            @pl.when(o == e)
-            def _():
-                own_copy.start()
+        square_send[...] = extra.astype(jnp.bfloat16).reshape(square_send.shape)
+        for q in range(8):
+            @pl.when(q != spot)
+            def _(q=q):
+                square_copy(q).start()
+
+        own_squares.start()
 
     def finish_decode():
         own_copy.wait()
-
-        @pl.loop(1, N_E)
+        own_squares.wait()
+        for q in range(8):
+            @pl.when(q != spot)
+            def _(q=q):
+                pltpu.make_async_copy(square_send.at[q], square_out.at[q], r_square.at[q]).wait()
+                square_copy(q).wait_send()
+
+        for group in range(4):
+            pair_copy(group).wait_send()
+
+        @pl.loop(1, N_E // 2)
         def _(i):
-            source = (e + i) % N_E
-            pltpu.make_async_copy(pre_send.at[source], pre_out.at[source], r_pre.at[source]).wait()
+            source = (plane_spot + i) % (N_E // 2)
+            pltpu.make_async_copy(pair_sum.at[source], pre_out.at[source], r_pre.at[source]).wait()
             pre_copy(source).wait_send()
 
         @pl.when(sends_hidden)
@@ -457,82 +541,106 @@
         for half in (0, 1):
             for i in range(1, 8):
                 ctx_copy(half, i).wait_send()
-            for d in (1, 2, 3):
+            for d in (1, 3):
                 row_copy(half, d).wait_send()
+                relay_copy(half, d).wait_send()
         for j in (1, 2, 3):
             part_copy(j).wait_send()
-            held_copy(j).wait_send()
-        for k in range(4):
-            target, copy = msg_copy(k)
+            held_copy(j - 1).wait_send()
+        for column in range(4):
+            target, copy = msg_copy(column)
 
             @pl.when(target != e)
             def _(copy=copy):
                 copy.wait_send()
-
-    n_parts = range(len(PARTS))
-    z_parts = [p for p in n_parts if PARTS[p][1]]
-    flat_parts = [p for p in n_parts if not PARTS[p][1]]
+        for d in (1, 2, 3):
+            lift_copy(d).wait_send()
+
     ctx_start()
-    optimize()
+    optimize(0, EARLY)
+    near_start("z", "own+", "own-")
+    optimize(EARLY, blocks - EARLY)
     row_start()
-    near_start("z")
-    near_start("own+", "own-")
+    near_start("z b", "own+ b", "own- b")
     make_table()
     prepare()
     hid_start()
-    for p in z_parts:
-        pick(p, 0)
+    row_on()
+    pick(0, 0)
+    pick(1, 0)
     ctx_wait()
     project()
-    for p in flat_parts:
-        pick(p, 0)
-    for p in z_parts:
-        near_copy(p, "z").wait_recv()
-        near_copy(p, "z+").start()
-        near_copy(p, "z-").start()
+    near_wait(0, "z")
+    near_copy(0, "z+").start()
+    near_copy(0, "z-").start()
+    near_wait(1, "z")
+    near_copy(1, "z+").start()
+    near_copy(1, "z-").start()
     residual()
     msg_start()
-    for p in n_parts:
-        near_copy(p, "own+").wait_recv()
-        near_copy(p, "on+").start()
-    for p in flat_parts:
-        near_copy(p, "own-").wait_recv()
-        near_copy(p, "on-").start()
-    for p in z_parts:
-        pick(p, 0, 1)
+    near_wait(0, "own+")
+    near_copy(0, "on+").start()
+    near_wait(1, "own+")
+    near_copy(1, "on+").start()
+    near_wait(2, "own+")
+    near_copy(2, "on+").start()
+    near_wait(3, "own+")
+    near_copy(3, "on+").start()
+    near_wait(2, "own-")
+    near_copy(2, "on-").start()
+    near_wait(3, "own-")
+    near_copy(3, "on-").start()
+    pick(2, 0)
+    pick(3, 0)
+    msg_on()
+    pick(0, 0, 1)
+    pick(1, 0, 1)
+    pick(2, 1)
     msg_wait()
     held_start()
-    for p in z_parts:
-        near_copy(p, "z-").wait_recv()
-        near_copy(p, "on-").start()
-    for p in z_parts:
-        pick(p, 3)
-    for p in z_parts:
-        near_copy(p, "own-").wait_recv()
-        pick(p, 1)
+    near_wait(0, "z-")
+    near_copy(0, "on-").start()
+    near_wait(1, "z-")
+    near_copy(1, "on-").start()
+    pick(0, 3)
+    pick(1, 3)
+    pick(3, 1)
+    held_on()
+    near_wait(0, "own-")
+    pick(0, 1)
+    near_wait(1, "own-")
+    pick(1, 1)
     expert_rows(0)
     expert_rows(1)
     expert_rows(2)
     expert_rows(3)
-    for p in flat_parts:
-        pick(p, 1)
-        pick(p, 3)
-    for p in z_parts:
-        pick(p, 1, 1)
-    for p in z_parts:
-        near_copy(p, "z+").wait_recv()
-        pick(p, 3, 1)
-    for p in flat_parts:
-        near_copy(p, "on+").wait_recv()
-        near_copy(p, "on-").wait_recv()
-        pick(p, 2)
-    for p in z_parts:
-        near_copy(p, "on+").wait_recv()
-        pick(p, 2)
-    for p in z_parts:
-        near_copy(p, "on-").wait_recv()
-        pick(p, 2, 1)
-
+    squares_start()
+    pick(0, 1, 1)
+    pick(1, 1, 1)
+    pick(2, 3)
+    expert_sums(0)
+    expert_sums(1)
+    expert_sums(2)
+    expert_sums(3)
+    pick(3, 3)
+    near_wait(0, "z+")
+    pick(0, 3, 1)
+    near_wait(1, "z+")
+    pick(1, 3, 1)
+    near_wait(2, "on+")
+    near_wait(2, "on-")
+    pick(2, 2)
+    near_wait(3, "on+")
+    near_wait(3, "on-")
+    pick(3, 2)
+    near_wait(0, "on+")
+    pick(0, 2)
+    near_wait(1, "on+")
+    pick(1, 2)
+    near_wait(0, "on-")
+    pick(0, 2, 1)
+    near_wait(1, "on-")
+    pick(1, 2, 1)
     optimize_end()
     finish_decode()
     rollout_end()
@@ -550,12 +658,13 @@
     return pl.pallas_call(
         step_kernel,
         out_shape=(
-            jax.ShapeDtypeStruct((N_E, TOK_DEV, MSG), bf16),
+            jax.ShapeDtypeStruct((N_E // 2, TOK_DEV, FCOL), bf16),
+            jax.ShapeDtypeStruct((8, TOK_DEV, GROUP), bf16),
             jax.ShapeDtypeStruct((4, 4, 2, CAP, block_rows, columns), bf16),
             state, state, state,
         ),
         in_specs=[anywhere] * 8 + [vmem],
-        out_specs=(anywhere,) * 5,
+        out_specs=(anywhere,) * 6,
         scratch_shapes=[
             pltpu.SMEM((N_E, 128), jnp.int32),
             pltpu.VMEM(master.shape, bf16),
@@ -576,13 +685,17 @@
             pltpu.VMEM((N_T, GROUP, WIDE), bf16),
             pltpu.VMEM((N_T, GROUP, WIDE), bf16),
             pltpu.VMEM((GROUP, WIDE), jnp.float32),
-            pltpu.VMEM((GROUP, WIDE), bf16),
+            pltpu.VMEM((4, GROUP, WIDE), bf16),
             pltpu.VMEM((N_T, 4, GROUP, WIDE), bf16),
-            pltpu.VMEM((N_E, TOK_DEV, MSG), bf16),
+            pltpu.VMEM((N_E // 2, 2, TOK_DEV, FCOL), bf16),
+            pltpu.VMEM((N_E // 2, TOK_DEV, FCOL), bf16),
+            pltpu.VMEM((N_E // 2, TOK_DEV, FCOL), bf16),
+            dma((4,)), dma((4,)),
             dma((16,)), dma((16,)), dma((8,)), dma((8,)),
-            dma((N_E,)), dma((8,)), dma((N_T,)), dma((N_T,)), dma((4,)), dma((4,)),
-            dma((N_T,)), dma((N_T,)), dma((N_E,)), dma((N_E,)), dma,
-            dma((32,)), dma((32,)), dma((128,)), dma((128,)),
+            dma((N_E,)), dma((8,)), dma((N_T,)), dma((N_T,)), dma((4,)), dma((4,)), dma((4,)), dma((4,)),
+            dma((3,)), dma((3,)), dma((N_E // 2,)), dma((N_E // 2,)), dma((2,)),
+            pltpu.VMEM((8, TOK_DEV, GROUP), bf16), dma((8,)), dma((8,)),
+            dma((40,)), dma((40,)), dma((128,)), dma((128,)),
             *[pltpu.VMEM((32, CAP, rows, columns), bf16) for _, _, _, rows in PARTS],
             *[
                 pltpu.VMEM((blocks, rows, columns), bf16)
@@ -600,9 +713,9 @@
 
 
 def finish_kernel(
-    plan, route, partial_in, roll, master_in, first_in, second_in,
+    plan_in, route_in, partial_in, squares_in, roll, master_in, first_in, second_in,
     out, rollout, master, first, second,
-    stage, state, partial, seen, in_sems, out_sems, state_in_sems, state_out_sems, partial_sem,
+    plan, route, stage, state, partial, square_parts, seen, in_sems, out_sems, state_in_sems, state_out_sems, decode_sems,
 ):
     e = lax.axis_index("expert")
     slots = rollout.shape[0]
@@ -620,14 +733,21 @@
     def state_out(i):
         return pltpu.make_async_copy(state.at[i], targets[i], state_out_sems.at[i])
 
-    partial_copy = pltpu.make_async_copy(partial_in, partial, partial_sem)
-    partial_copy.start()
+    partial_copy = pltpu.make_async_copy(partial_in, partial, decode_sems.at[0])
+    squares_copy = pltpu.make_async_copy(squares_in, square_parts, decode_sems.at[1])
+    plan_copy = pltpu.make_async_copy(plan_in, plan, decode_sems.at[2])
+    route_copy = pltpu.make_async_copy(route_in, route, decode_sems.at[3])
+    plan_copy.start()
+    route_copy.start()
     for i in range(3):
         state_in(i).start()
 
     @pl.loop(0, N_E)
     def _(j):
         seen[j] = 0
+
+    plan_copy.wait()
+    route_copy.wait()
 
     @pl.loop(0, slots)
     def _(j):
@@ -639,6 +759,8 @@
         dz = (source + e) % 2
         fetch(j, ((dx * 4 + dy) * 2 + dz) * CAP + rank).start()
 
+    partial_copy.start()
+    squares_copy.start()
     for i in range(3):
         state_in(i).wait()
         state_out(i).start()
@@ -649,6 +771,7 @@
         store(j).start()
 
     partial_copy.wait()
+    squares_copy.wait()
     token = lax.broadcasted_iota(jnp.int32, (TOK_DEV, 1), 0)
     expert = jnp.zeros((TOK_DEV, 1), jnp.int32)
     for i in range(TOK_DEV):
@@ -657,11 +780,11 @@
     squares = jnp.zeros((TOK_DEV, 1), jnp.float32)
     for k in range(4):
         total = jnp.zeros((TOK_DEV, FCOL), jnp.float32)
-        for h in range(8):
-            total = total + partial[k * 8 + h, :, :FCOL].astype(jnp.float32)
+        for h in range(4):
+            total = total + partial[k * 4 + h].astype(jnp.float32)
         pre = pre + jnp.where(expert == k, total, 0.0)
     for h in range(8):
-        squares = squares + jnp.sum(partial[h, :, FCOL:].astype(jnp.float32), axis=1, keepdims=True)
+        squares = squares + jnp.sum(square_parts[h].astype(jnp.float32), axis=1, keepdims=True)
     pre = pre * lax.rsqrt(squares / (N_E * COLS) + 1e-06)
     out[...] = (pre / (1.0 + jnp.exp(-pre))).astype(jnp.bfloat16)
 
@@ -673,9 +796,8 @@
         state_out(i).wait()
 
 
-def finish(plan, route, partial, roll, state):
+def finish(plan, route, partial, squares, roll, state):
     vmem = pl.BlockSpec(memory_space=pltpu.VMEM)
-    smem = pl.BlockSpec(memory_space=pltpu.SMEM)
     anywhere = pl.BlockSpec(memory_space=pl.ANY)
     block_rows, columns = roll.shape[-2:]
     slots = plan.shape[0] // N_E
@@ -688,27 +810,30 @@
             jax.ShapeDtypeStruct((slots, block_rows, columns), jnp.bfloat16),
             shape, shape, shape,
         ),
-        in_specs=[smem, smem] + [anywhere] * 5,
+        in_specs=[anywhere] * 8,
         out_specs=(vmem,) + (anywhere,) * 4,
         scratch_shapes=[
+            pltpu.SMEM(plan.shape, jnp.int32),
+            pltpu.SMEM(route.shape, jnp.int32),
             pltpu.VMEM((slots, block_rows, columns), jnp.bfloat16),
             pltpu.VMEM((3, *state[0].shape), jnp.float32),
             pltpu.VMEM(partial.shape, partial.dtype),
+            pltpu.VMEM(squares.shape, squares.dtype),
             pltpu.SMEM((N_E,), jnp.int32),
-            dma((slots,)), dma((slots,)), dma((3,)), dma((3,)), dma,
+            dma((slots,)), dma((slots,)), dma((3,)), dma((3,)), dma((4,)),
         ],
         compiler_params=pltpu.CompilerParams(vmem_limit_bytes=56 * 2**20),
         name="finish",
-    )(plan, route, partial, roll.reshape(4 * 4 * 2 * CAP, block_rows, columns), *state)
+    )(plan, route, partial, squares, roll.reshape(4 * 4 * 2 * CAP, block_rows, columns), *state)
 
 
 def shards(
     master, grad, moment_one, moment_two, context, out_weight, hidden, norm_gain, route, plan
 ):
-    partial, roll, *state = step(
+    partial, squares, roll, *state = step(
         master, grad, moment_one, moment_two, context, out_weight, hidden, norm_gain, plan
     )
-    activation, rollout, *state = finish(plan, route, partial, roll, state)
+    activation, rollout, *state = finish(plan, route, partial, squares, roll, state)
     return (*state, rollout, activation)
 
 

time: 127 us -> 112 us (0.88); the launches traced: 127 us -> 110 us
  Pallas kernels: 126 us -> 110 us
    pallas_call x1, Pallas kernels: 116 us -> 102 us  [step(): pl.pallas_call(step_kernel, out_shape=(jax.ShapeDtypeStruct((N_E // 2, TO...]
    pallas_call x1, Pallas kernels: 9.73 us -> 7.85 us  [finish(): pl.pallas_call(finish_kernel, out_shape=(jax.ShapeDtypeStruct((TOK_DEV, F...]
where the time goes in v4:
time: 112 us; the launch traced here: 110 us
  Pallas kernels  110 us (98%)
    pallas_call x1, Pallas kernels, step(): pl.pallas_call(step_kernel, out_shape=(jax.ShapeDtypeStruct((N_E // 2, TO...  102 us
    pallas_call x1, Pallas kernels, finish(): pl.pallas_call(finish_kernel, out_shape=(jax.ShapeDtypeStruct((TOK_DEV, F...  7.85 us

profile of v4, /device:TPU:0, one launch (start us, length us, event | category | flops | bytes accessed | tf_op | source)
XLA Modules:
  0.0 110.3 jit_solution(12633018304008743721)
XLA Ops:
  0.6 101.8 %step.1 = (bf16[16,16,512]{2,1,0:T(8,128)(2,1)}, bf16[8,16,128]{2,1,0:T(8,128)(2,1)}, bf16[4,4,2,2,128,512]{5,4,3,2,1,0:T(8,128)(2,1)}, f32[7,128,512]{2,1,0:T(8...) custom-call(f32[7,128,512]{2,1,0:T(8,128)} %master.1, bf16[7,128,512]{2,1,0:T(8,128)(2,1)} %grad.1, ...), custom_call_target="tpu_custom_call" | custom-call | tf_op jit(solution)/shard_map/step/pallas_call | solution.py:658
  102.4 7.8 %finish.1 = (bf16[16,512]{1,0:T(8,128)(2,1)}, bf16[32,128,512]{2,1,0:T(8,128)(2,1)}, f32[7,128,512]{2,1,0:T(8,128)}, f32[7,128,512]{2,1,0:T(8,128)}, f32[7,128,512]{2,1,0:T(8,128)}) custom-call(s32[1024]{0:T(1024)} %plan_in.1, s32[512]{0:T(512)} %route_in.1, bf16[16,16,512]{2,1,0:T(8,128)(2,1)} %get-tuple-element.16.partial_in, ...), custom_call_target="tpu_custom_call" | custom-call | tf_op jit(solution)/shard_map/finish/pallas_call | solution.py:806

commit v5 on v4

--- a/solution.py
+++ b/solution.py
@@ -45,10 +45,10 @@
 
 
 def step_kernel(
-    master, grad, first, second, ctx, ow_in, hid_in, gain_in, plan,
+    master, grad, first, second, ctx, ow_in, hid_in, gain_in, plan_in,
     pre_out, square_out, roll, new_master, new_first, new_second,
     table, cast, state_in, grad_in, state_out, sent_index, s_state, s_grad, s_out, s_table,
-    ow, hid, gain, s_load, ctx_all,
+    ow, hid, gain, plan, s_load, ctx_all,
     ow_wide, hid_send, hid_recv, gain_all, part_send, part_recv, part_own, msg, held, pre_send, pair_recv, pair_sum, s_pair, r_pair,
     s_ctx, r_ctx, s_row, r_row, s_hid, r_hid, s_part, r_part, s_lift, r_lift, s_msg, r_msg, s_held, r_held, s_pre, r_pre, local_sem,
     square_send, s_square, r_square, s_near, r_near, s_pick, r_pick, *rest
@@ -64,9 +64,18 @@
     t = lax.axis_index("tensor")
     y, x, z = e // 8, (e // 2) % 4, e % 2
 
+    barrier = pltpu.get_barrier_semaphore()
+
+    @pl.loop(1, N_E)
+    def _(i):
+        pl.semaphore_signal(barrier, 1, device_id=((e + i) % N_E, t), device_id_type=MESH)
+
+    for j in range(1, N_T):
+        pl.semaphore_signal(barrier, 1, device_id=(e, (t + j) % N_T), device_id_type=MESH)
+
     loads = [
         pltpu.make_async_copy(source, target, s_load.at[i])
-        for i, (source, target) in enumerate(((ow_in, ow), (hid_in, hid), (gain_in, gain)))
+        for i, (source, target) in enumerate(((ow_in, ow), (hid_in, hid), (gain_in, gain), (plan_in, plan)))
     ]
     for load in loads:
         load.start()
@@ -86,15 +95,8 @@
             state_copy(b, i).start()
         grad_copy(b).start()
 
-    barrier = pltpu.get_barrier_semaphore()
-
-    @pl.loop(1, N_E)
-    def _(i):
-        pl.semaphore_signal(barrier, 1, device_id=((e + i) % N_E, t), device_id_type=MESH)
-
-    for j in range(1, N_T):
-        pl.semaphore_signal(barrier, 1, device_id=(e, (t + j) % N_T), device_id_type=MESH)
-    pl.semaphore_wait(barrier, N_E - 1 + N_T - 1)
+    def barrier_wait():
+        pl.semaphore_wait(barrier, N_E - 1 + N_T - 1)
 
     def at(dy, dx, dz):
         return ((y + dy) % 4) * 8 + ((x + dx) % 4) * 2 + (z + dz) % 2
@@ -238,6 +240,7 @@
     table_copy = pltpu.make_async_copy(sent_index, table, s_table)
 
     def make_table():
+        loads[3].wait()
         wanted = plan[...]
         source = (wanted * 9363) >> 16
         local = wanted - source * blocks
@@ -556,8 +559,9 @@
         for d in (1, 2, 3):
             lift_copy(d).wait_send()
 
+    optimize(0, EARLY)
+    barrier_wait()
     ctx_start()
-    optimize(0, EARLY)
     near_start("z", "own+", "own-")
     optimize(EARLY, blocks - EARLY)
     row_start()
@@ -590,21 +594,21 @@
     near_copy(2, "on-").start()
     near_wait(3, "own-")
     near_copy(3, "on-").start()
+    msg_on()
     pick(2, 0)
     pick(3, 0)
-    msg_on()
     pick(0, 0, 1)
     pick(1, 0, 1)
-    pick(2, 1)
     msg_wait()
     held_start()
+    pick(2, 1)
+    pick(3, 1)
     near_wait(0, "z-")
     near_copy(0, "on-").start()
     near_wait(1, "z-")
     near_copy(1, "on-").start()
     pick(0, 3)
     pick(1, 3)
-    pick(3, 1)
     held_on()
     near_wait(0, "own-")
     pick(0, 1)
@@ -647,7 +651,6 @@
 
 
 def step(master, grad, first, second, context, out_weight, hidden, norm_gain, plan):
-    vmem = pl.BlockSpec(memory_space=pltpu.VMEM)
     anywhere = pl.BlockSpec(memory_space=pl.ANY)
     dma = pltpu.SemaphoreType.DMA
     bf16 = jnp.bfloat16
@@ -663,7 +666,7 @@
             jax.ShapeDtypeStruct((4, 4, 2, CAP, block_rows, columns), bf16),
             state, state, state,
         ),
-        in_specs=[anywhere] * 8 + [vmem],
+        in_specs=[anywhere] * 9,
         out_specs=(anywhere,) * 6,
         scratch_shapes=[
             pltpu.SMEM((N_E, 128), jnp.int32),
@@ -676,7 +679,8 @@
             pltpu.VMEM((COLS, depth), bf16),
             pltpu.VMEM((TOK_DEV, width), bf16),
             pltpu.VMEM((1, width), jnp.float32),
-            dma((3,)),
+            pltpu.VMEM((8, 128), jnp.int32),
+            dma((4,)),
             pltpu.VMEM((2, 4, 4, 2, TOK_DEV, depth // 2), bf16),
             pltpu.VMEM((WIDE, depth), bf16),
             pltpu.VMEM((N_E, TOK_DEV, WIDE), bf16),

time: 112 us -> 110 us (0.982)
  Pallas kernels: 110 us -> 108 us
    pallas_call x1, Pallas kernels: 102 us -> 100 us  [step(): pl.pallas_call(step_kernel, out_shape=(jax.ShapeDtypeStruct((N_E // 2, TO...]
where the time goes in v5:
time: 110 us; the launch traced here: 108 us
  Pallas kernels  108 us (98%)
    pallas_call x1, Pallas kernels, step(): pl.pallas_call(step_kernel, out_shape=(jax.ShapeDtypeStruct((N_E // 2, TO...  100 us
    pallas_call x1, Pallas kernels, finish(): pl.pallas_call(finish_kernel, out_shape=(jax.ShapeDtypeStruct((TOK_DEV, F...  7.85 us

profile of v5, /device:TPU:0, one launch (start us, length us, event | category | flops | bytes accessed | tf_op | source)
XLA Modules:
  0.0 108.5 jit_solution(3039415478720901668)
XLA Ops:
  0.6 100.0 %step.1 = (bf16[16,16,512]{2,1,0:T(8,128)(2,1)}, bf16[8,16,128]{2,1,0:T(8,128)(2,1)}, bf16[4,4,2,2,128,512]{5,4,3,2,1,0:T(8,128)(2,1)}, f32[7,128,512]{2,1,0:T(8...) custom-call(f32[7,128,512]{2,1,0:T(8,128)} %master.1, bf16[7,128,512]{2,1,0:T(8,128)(2,1)} %grad.1, ...), custom_call_target="tpu_custom_call" | custom-call | tf_op jit(solution)/shard_map/step/pallas_call | solution.py:661
  100.6 7.8 %finish.1 = (bf16[16,512]{1,0:T(8,128)(2,1)}, bf16[32,128,512]{2,1,0:T(8,128)(2,1)}, f32[7,128,512]{2,1,0:T(8,128)}, f32[7,128,512]{2,1,0:T(8,128)}, f32[7,128,512]{2,1,0:T(8,128)}) custom-call(s32[1024]{0:T(1024)} %plan_in.1, s32[512]{0:T(512)} %route_in.1, bf16[16,16,512]{2,1,0:T(8,128)(2,1)} %get-tuple-element.16.partial_in, ...), custom_call_target="tpu_custom_call" | custom-call | tf_op jit(solution)/shard_map/finish/pallas_call | solution.py:810

commit v6 on v5

--- a/solution.py
+++ b/solution.py
@@ -199,8 +199,9 @@
         for p in range(len(PARTS)):
             for step in steps_of(p):
                 near_copy(p, step).wait_send()
-            for d in range(4):
-                for dz in (0, 1) if PARTS[p][1] else (0,):
+        for d, dz in ((0, 0), (0, 1), (1, 0), (3, 0), (1, 1), (3, 1), (2, 0), (2, 1)):
+            for p in range(len(PARTS)):
+                if PARTS[p][1] or dz == 0:
                     for od, odz in targets(p):
                         pick_copy(p, d, dz, od, odz).wait()
 

time: 110 us -> 109 us (level)
  no operation moved by 1% of the time
where the time goes in v6:
time: 109 us; the launch traced here: 108 us
  Pallas kernels  108 us (99%)
    pallas_call x1, Pallas kernels, step(): pl.pallas_call(step_kernel, out_shape=(jax.ShapeDtypeStruct((N_E // 2, TO...  99.7 us
    pallas_call x1, Pallas kernels, finish(): pl.pallas_call(finish_kernel, out_shape=(jax.ShapeDtypeStruct((TOK_DEV, F...  7.85 us

profile of v6, /device:TPU:0, one launch (start us, length us, event | category | flops | bytes accessed | tf_op | source)
XLA Modules:
  0.0 108.2 jit_solution(4574881722432290269)
XLA Ops:
  0.6 99.7 %step.1 = (bf16[16,16,512]{2,1,0:T(8,128)(2,1)}, bf16[8,16,128]{2,1,0:T(8,128)(2,1)}, bf16[4,4,2,2,128,512]{5,4,3,2,1,0:T(8,128)(2,1)}, f32[7,128,512]{2,1,0:T(8...) custom-call(f32[7,128,512]{2,1,0:T(8,128)} %master.1, bf16[7,128,512]{2,1,0:T(8,128)(2,1)} %grad.1, ...), custom_call_target="tpu_custom_call" | custom-call | tf_op jit(solution)/shard_map/step/pallas_call | solution.py:662
  100.4 7.8 %finish.1 = (bf16[16,512]{1,0:T(8,128)(2,1)}, bf16[32,128,512]{2,1,0:T(8,128)(2,1)}, f32[7,128,512]{2,1,0:T(8,128)}, f32[7,128,512]{2,1,0:T(8,128)}, f32[7,128,512]{2,1,0:T(8,128)}) custom-call(s32[1024]{0:T(1024)} %plan_in.1, s32[512]{0:T(512)} %route_in.1, bf16[16,16,512]{2,1,0:T(8,128)(2,1)} %get-tuple-element.16.partial_in, ...), custom_call_target="tpu_custom_call" | custom-call | tf_op jit(solution)/shard_map/finish/pallas_call | solution.py:811
